TPU v7x, 256 devices: a whole 4x4x8 slice. The times are simulated.
256 devices in a mesh: outer: 16 (over x, y_lo, core), inner: 16 (over z, y_hi).
Axes of the slice: x: 4, y: 4 (y_hi: 2, y_lo: 2; y = y_hi * 2 + y_lo), z: 8, core: 2. Of those that a mesh axis runs over, the one named last changes fastest.
Arguments:
- queries: bfloat16 [98304, 1024], P(('outer', 'inner')), may hold values from -4.6 to 4.6
- keys: bfloat16 [98304, 128], P(('outer', 'inner')), may hold values from -4.6 to 4.6
- values: bfloat16 [98304, 128], P(('outer', 'inner')), may hold values from -5 to 5
- grad_out: bfloat16 [98304, 1024], P(('outer', 'inner')), may hold values from -5 to 5
- span_order: int32 [512], replicated, may hold values from 0 to 511, each once
Outputs:
- grad_queries: bfloat16 [98304, 1024], P(('outer', 'inner'))
- grad_keys: bfloat16 [98304, 128], P(('outer', 'inner'))
- grad_values: bfloat16 [98304, 128], P(('outer', 'inner'))
Inputs may be any that keep to these rules, and one draw needn't show every extreme that they name: `span_order`: A permutation: every span number appears once.
All inputs are finite; a program needn't handle non-finite values.
Results may differ from a plain program's by a relative error of at most 0.011.
Values may be sent and summed in bfloat16 or wider, within the bound.
No kernel may reach another device: no remote copies, remote signals or barrier semaphores. Data moves between devices by JAX's collectives and lax.ppermute only.
A program may use at most 128 MiB of HBM per device.

v0:
```python
import math

import jax
import jax.numpy as jnp
from jax import lax
from jax.sharding import PartitionSpec as P

HEADS = 8
HEAD = 128
STEPS = 4


def shifted(value, axis, by):
    size = lax.axis_size(axis)
    return lax.ppermute(value, axis, [(i, (i + by) % size) for i in range(size)])


def window_attention(query_rows, key_value, grad_rows, query_pos, key_pos):
    inv_root = 1.0 / math.sqrt(HEAD)
    tok_rows = query_rows.shape[0]
    query_heads = query_rows.reshape(tok_rows, HEADS, HEAD)
    grad_heads = grad_rows.reshape(tok_rows, HEADS, HEAD)
    key_part = key_value[:, :HEAD]
    value_part = key_value[:, HEAD:]
    scores = (
        jnp.einsum("thd,kd->htk", query_heads, key_part, preferred_element_type=jnp.float32)
        * inv_root
    )
    visible = key_pos[None, :] <= query_pos[:, None]
    scores = jnp.where(visible[None], scores, -jnp.inf)
    row_max = jnp.max(scores, axis=2, keepdims=True)
    log_total = row_max + jnp.log(jnp.sum(jnp.exp(scores - row_max), axis=2, keepdims=True))
    probability = jnp.exp(scores - log_total)
    prob_round = probability.astype(jnp.bfloat16)
    attended = jnp.einsum(
        "htk,kd->thd", prob_round, value_part, preferred_element_type=jnp.float32
    ).astype(jnp.bfloat16)
    attended_f = lax.optimization_barrier(attended).astype(jnp.float32)
    row_dot = jnp.sum(grad_heads.astype(jnp.float32) * attended_f, axis=2)
    grad_prob = jnp.einsum(
        "thd,kd->htk", grad_heads, value_part, preferred_element_type=jnp.float32
    )
    grad_score = probability * (grad_prob - jnp.transpose(row_dot)[:, :, None]) * inv_root
    score_round = grad_score.astype(jnp.bfloat16)
    grad_q = jnp.einsum("htk,kd->thd", score_round, key_part, preferred_element_type=jnp.float32)
    grad_q = grad_q.reshape(tok_rows, HEADS * HEAD).astype(jnp.bfloat16)
    grad_k = jnp.einsum("htk,thd->kd", score_round, query_heads, preferred_element_type=jnp.float32)
    grad_v = jnp.einsum("htk,thd->kd", prob_round, grad_heads, preferred_element_type=jnp.float32)
    return (grad_q, jnp.concatenate([grad_k, grad_v], axis=1))


def body(queries, keys, values, grad_out, span_order):
    inner_count = lax.axis_size("inner")
    outer_count = lax.axis_size("outer")
    outer_index = lax.axis_index("outer")
    inner_index = lax.axis_index("inner")
    tok_rows = queries.shape[0]
    span_len = tok_rows // 2
    key_value = jnp.concatenate([keys, values], axis=1)
    arrived = [key_value]
    moving = key_value
    for stride in range(1, STEPS):
        moving = shifted(moving, "inner", 1)
        arrived.append(moving)
    arrived.append(shifted(key_value, "outer", 1))
    block_list = [
        outer_index * inner_count + (inner_index - stride) % inner_count for stride in range(STEPS)
    ]
    block_list.append((outer_index - 1) % outer_count * inner_count + inner_index)
    offsets = jnp.arange(span_len, dtype=jnp.int32)

    def positions_of(block_id):
        slots = lax.dynamic_slice_in_dim(span_order, 2 * block_id, 2, 0)
        return (slots[:, None] * span_len + offsets[None, :]).reshape(-1)

    key_pos = jnp.concatenate([positions_of(other) for other in block_list], axis=0)
    query_pos = positions_of(block_list[0])
    grad_q, partial_value = window_attention(
        queries, jnp.concatenate(arrived, axis=0), grad_out, query_pos, key_pos
    )
    pieces = [
        partial_value[number * tok_rows : (number + 1) * tok_rows] for number in range(STEPS + 1)
    ]
    summed = pieces[STEPS - 1]
    for stride in range(STEPS - 2, -1, -1):
        summed = shifted(summed, "inner", -1) + pieces[stride]
    summed = summed + shifted(pieces[STEPS], "outer", -1)
    return (grad_q, summed[:, :HEAD].astype(jnp.bfloat16), summed[:, HEAD:].astype(jnp.bfloat16))


def solution(mesh):
    placed = (
        P(("outer", "inner"), None),
        P(("outer", "inner"), None),
        P(("outer", "inner"), None),
        P(("outer", "inner"), None),
        P(),
    )
    return jax.shard_map(
        body,
        mesh=mesh,
        in_specs=placed,
        out_specs=(
            P(("outer", "inner"), None),
            P(("outer", "inner"), None),
            P(("outer", "inner"), None),
        ),
        check_vma=False,
    )
```

profile of v0, /device:TPU:123, one launch (start us, length us, event | category | flops | bytes accessed | tf_op | source)
XLA Modules:
  0.0 138.2 jit_solution(1321433587092858611)
XLA Ops:
  0.6 1.6 %constant_dynamic-update-slice_fusion.1 = (bf16[384,256]{1,0:T(8,128)(2,1)}, bf16[1920,256]{1,0:T(8,128)(2,1)S(1)}) fusion(bf16[384,128]{1,0:T(8,128)(2,1)} %param.6), kind=kLoop, calls=%fused_computation.38 | loop fusion | bytes 294912
  2.2 1.6 %constant_dynamic-update-slice_fusion = (bf16[384,256]{1,0:T(8,128)(2,1)}, bf16[1920,256]{1,0:T(8,128)(2,1)S(1)}) fusion(bf16[384,256]{1,0:T(8,128)(2,1)} %get-tuple-element.12, bf16[384,128]{1,0:T(8,128)(2,1)} %param.7, bf16[1920,256]{1,0:T(8,128)(2,1)S(1)} %get-tuple-element.13), kind=kLoop, calls=%fused_computation.37 | loop fusion | bytes 294912 | tf_op jit(solution)/shard_map/concatenate | solution.py:59
  3.7 3.5 %collective-permute-start = (bf16[384,256]{1,0:T(8,128)(2,1)}, bf16[384,256]{1,0:T(8,128)(2,1)}, u32[]{:S(2)}, u32[]{:S(2)}) collective-permute-start(bf16[384,256]{1,0:T(8,128)(2,1)} %get-tuple-element.10), channel_id=1, source_target_pairs={{0,1},{1,2},{2,3},{3,4},{4,5},{5,6},{6,7},{7,8},{8,9},{9,10},{10,1... | collective-permute-start | bytes 589832 | tf_op jit(solution)/shard_map/ppermute | solution.py:15
  7.3 1.3 collective-permute-start.3
  8.6 0.9 dynamic-slice_multiply_fusion
  9.5 0.1 iota_add_fusion.4
  9.6 0.1 add.173
  9.7 0.1 iota_add_fusion.2
  9.8 0.1 add.180
  9.9 0.1 add.187
  9.9 0.1 iota_add_fusion
  10.0 0.1 add.194
  10.1 0.1 add.201
  10.2 3.2 %collective-permute-done = bf16[384,256]{1,0:T(8,128)(2,1)} collective-permute-done((bf16[384,256]{1,0:T(8,128)(2,1)}, bf16[384,256]{1,0:T(8,128)(2,1)}, u32[]{:S(2)}, u32[]{:S(2)}) %collective-permute-start) | collective-permute-done | bytes 196640 | tf_op jit(solution)/shard_map/ppermute | solution.py:15
  13.4 5.0 %collective-permute-start.1 = (bf16[384,256]{1,0:T(8,128)(2,1)}, bf16[384,256]{1,0:T(8,128)(2,1)}, u32[]{:S(2)}, u32[]{:S(2)}) collective-permute-start(bf16[384,256]{1,0:T(8,128)(2,1)} %collective-permute-done), channel_id=1, source_target_pairs={{0,1},{1,2},{2,3},{3,4},{4,5},{5,6},{6,7},{7,8},{8,9},{9,10},{10,1... | collective-permute-start | bytes 589832 | tf_op jit(solution)/shard_map/ppermute | solution.py:15
  18.4 0.9 broadcast_compare_fusion
  19.4 1.5 %copy.30 = bf16[384,1024]{0,1:T(8,128)(2,1)S(1)} copy(bf16[384,1024]{1,0:T(8,128)(2,1)} %param.5) | data formatting | bytes 1572864 | tf_op jit(solution)/shard_map/reshape | solution.py:21
  20.9 1.5 %copy.9 = bf16[384,1024]{0,1:T(8,128)(2,1)S(1)} copy(bf16[384,1024]{1,0:T(8,128)(2,1)} %param.8) | data formatting | bytes 1572864 | tf_op args[3]
  22.3 0.0 collective-permute-done.1
  22.4 4.5 %collective-permute-start.2 = (bf16[384,256]{1,0:T(8,128)(2,1)}, bf16[384,256]{1,0:T(8,128)(2,1)S(1)}, u32[]{:S(2)}, u32[]{:S(2)}) collective-permute-start(bf16[384,256]{1,0:T(8,128)(2,1)} %collective-permute-done.1), channel_id=1, source_target_pairs={{0,1},{1,2},{2,3},{3,4},{4,5},{5,6},{6,7},{7,8},{8,9},{9,10},{10,1... | collective-permute-start | bytes 589832 | tf_op jit(solution)/shard_map/ppermute | solution.py:15
  26.9 0.9 constant_dynamic-update-slice_fusion.5
  27.8 0.9 constant_dynamic-update-slice_fusion.4
  28.8 1.0 collective-permute-done.2
  29.8 0.0 collective-permute-done.3
  29.9 0.0 copy-start.1
  29.9 3.6 %fusion.4 = (f32[8,384]{1,0:T(8,128)S(1)}, f32[1920,384,8]{1,0,2:T(8,128)S(1)}) fusion(pred[384,1920]{0,1:T(8,128)(4,1)S(1)} %broadcast_compare_fusion, bf16[384,8,128]{0,2,1:T(8,128)(2,1)S(1)} %bitcast.53, bf16[1920,256]{1,0:T(8,128)(2,1)S(1)} %constant_dynamic-update-slice_fusion.2), kind=kOutput, calls=%fused_computation.8 | convolution fusion | flops 1527641088 | bytes 25620480 | tf_op jit(solution)/shard_map/thd,kd->htk/dot_general | solution.py:26
  33.5 0.0 copy-start
  33.5 7.8 %copy-done = f32[1920,384,8]{1,0,2:T(8,128)} copy-done((f32[1920,384,8]{1,0,2:T(8,128)}, f32[1920,384,8]{1,0,2:T(8,128)S(1)}, u32[]{:S(2)}) %copy-start) | copy-done | bytes 23592984
  41.3 4.9 %exponential_reduce_fusion = f32[8,384]{1,0:T(8,128)S(1)} fusion(f32[1920,384,8]{1,0,2:T(8,128)S(1)} %get-tuple-element.20, f32[8,384]{1,0:T(8,128)S(1)} %get-tuple-element.19, pred[384,1920]{0,1:T(8,128)(4,1)S(1)} %broadcast_compare_fusion), kind=kLoop, calls=%fused_computation.6 | loop fusion | flops 23589888 | bytes 24354816 | tf_op jit(solution)/shard_map/reduce_sum | solution.py:32
  46.2 0.0 copy-done.1
  46.2 10.9 %fusion.5 = bf16[384,8,128]{0,2,1:T(8,128)(2,1)S(1)} fusion(bf16[1920,256]{1,0:T(8,128)(2,1)S(1)} %constant_dynamic-update-slice_fusion.2, f32[1920,384,8]{1,0,2:T(8,128)} %copy-done, f32[8,384]{1,0:T(8,128)S(1)} %log_add_fusion, pred[384,1920]{0,1:T(8,128)(4,1)S(1)} %broadcast_compare_fusion), kind=kOutput, calls=%fused_computation.23 | convolution fusion | flops 1533935616 | bytes 25620480 | tf_op jit(solution)/shard_map/htk,kd->thd/dot_general | solution.py:35
  57.2 0.2 multiply_reduce_fusion
  57.4 0.0 copy-start.2
  57.4 10.8 %convolution_bitcast_fusion = f32[1920,128]{0,1:T(8,128)S(1)} fusion(bf16[384,8,128]{0,2,1:T(8,128)(2,1)S(1)} %bitcast.56, f32[1920,384,8]{1,0,2:T(8,128)} %copy-done, f32[8,384]{1,0:T(8,128)S(1)} %log_add_fusion, pred[384,1920]{0,1:T(8,128)(4,1)S(1)} %broadcast_compare_fusion), kind=kOutput, calls=%fused_computation.17 | convolution fusion | flops 1533542400 | bytes 26112000 | tf_op jit(solution)/shard_map/htk,thd->kd/dot_general | solution.py:48
  68.3 0.0 copy-done.2
  68.3 16.8 %fusion.2 = bf16[8,384,1920]{1,2,0:T(8,128)(2,1)} fusion(f32[1920,384,8]{1,0,2:T(8,128)} %copy-done, f32[8,384]{1,0:T(8,128)S(1)} %bitcast.58, f32[8,384]{1,0:T(8,128)S(1)} %log_add_fusion, pred[384,1920]{0,1:T(8,128)(4,1)S(1)} %broadcast_compare_fusion, bf16[384,8,128]{0,2,1:T(8,128)(2,1)S(1)} %bitcast.57, bf16[1920,256]{1,0:T(8,128)(2,1)S(1)} %copy-done.2), kind=kOutput, calls=%fused_computation.3 | convolution fusion | flops 1551237120 | bytes 37429248 | tf_op jit(solution)/shard_map/thd,kd->htk/dot_general | solution.py:40
  85.1 0.0 slice-start
  85.1 0.0 slice-start.1
  85.1 8.3 %convolution_bitcast_fusion.1 = f32[1920,128]{0,1:T(8,128)S(1)} fusion(bf16[8,384,1920]{1,2,0:T(8,128)(2,1)} %fusion.2, bf16[384,8,128]{0,2,1:T(8,128)(2,1)S(1)} %bitcast.54), kind=kOutput, calls=%fused_computation.18 | convolution fusion | flops 1509949440 | bytes 13565952 | tf_op jit(solution)/shard_map/htk,thd->kd/dot_general | solution.py:47
  93.4 0.0 slice-start.2
  93.5 0.1 collective-permute-start.4
  93.6 10.6 %collective-permute-done.4 = f32[384,256]{0,1:T(8,128)S(1)} collective-permute-done((f32[384,256]{0,1:T(8,128)S(1)}, f32[384,256]{0,1:T(8,128)S(1)}, u32[]{:S(2)}, u32[]{:S(2)}) %collective-permute-start.4) | collective-permute-done | bytes 393248 | tf_op jit(solution)/shard_map/ppermute | solution.py:15
  104.2 0.1 fusion.12
  104.2 0.3 collective-permute-start.5
  104.5 10.2 %collective-permute-done.5 = f32[384,256]{0,1:T(8,128)S(1)} collective-permute-done((f32[384,256]{0,1:T(8,128)S(1)}, f32[384,256]{0,1:T(8,128)S(1)}, u32[]{:S(2)}, u32[]{:S(2)}) %collective-permute-start.5) | collective-permute-done | bytes 393248 | tf_op jit(solution)/shard_map/ppermute | solution.py:15
  114.8 0.1 fusion.14
  114.9 6.3 %collective-permute-start.7 = (f32[384,256]{0,1:T(8,128)S(1)}, f32[384,256]{0,1:T(8,128)}, u32[]{:S(2)}, u32[]{:S(2)}) collective-permute-start(f32[384,256]{0,1:T(8,128)S(1)} %get-tuple-element.7), channel_id=1, source_target_pairs={{0,240},{16,0},{32,16},{48,32},{64,48},{80,64},{96,80},{112,96},{1... | collective-permute-start | bytes 1179656 | tf_op jit(solution)/shard_map/ppermute | solution.py:15
  121.1 0.0 collective-permute-start.6
  121.1 0.0 slice-done
  121.1 0.0 slice-done.1
  121.1 0.0 slice-done.2
  121.2 1.8 %convolution_convert_fusion = bf16[128,8,384]{2,0,1:T(8,128)(2,1)S(1)} fusion(bf16[8,384,1920]{1,2,0:T(8,128)(2,1)S(1)} %bitcast.52, bf16[1920,256]{1,0:T(8,128)(2,1)S(1)} %copy-done.2), kind=kOutput, calls=%fused_computation.21 | convolution fusion | flops 1510342656 | bytes 13074432 | tf_op jit(solution)/shard_map/htk,kd->thd/dot_general | solution.py:45
  123.0 1.2 copy.18
  124.2 1.4 collective-permute-done.7
  125.6 10.0 %collective-permute-done.6 = f32[384,256]{0,1:T(8,128)} collective-permute-done((f32[384,256]{0,1:T(8,128)S(1)}, f32[384,256]{0,1:T(8,128)}, u32[]{:S(2)}, u32[]{:S(2)}) %collective-permute-start.6) | collective-permute-done | bytes 393248 | tf_op jit(solution)/shard_map/ppermute | solution.py:15
  135.5 1.2 fusion.9
  136.7 0.8 copy.19
  137.5 0.8 copy.20
  (12 shorter events, 0.1 us)
Async XLA Ops:
  3.7 9.7 %collective-permute-start = (bf16[384,256]{1,0:T(8,128)(2,1)}, bf16[384,256]{1,0:T(8,128)(2,1)}, u32[]{:S(2)}, u32[]{:S(2)}) collective-permute-start(bf16[384,256]{1,0:T(8,128)(2,1)} %get-tuple-element.10), channel_id=1, source_target_pairs={{0,1},{1,2},{2,3},{3,4},{4,5},{5,6},{6,7},{7,8},{8,9},{9,10},{10,1... | collective-permute-start | bytes 589832 | tf_op jit(solution)/shard_map/ppermute | solution.py:15
  7.3 22.6 %collective-permute-start.3 = (bf16[384,256]{1,0:T(8,128)(2,1)}, bf16[384,256]{1,0:T(8,128)(2,1)S(1)}, u32[]{:S(2)}, u32[]{:S(2)}) collective-permute-start(bf16[384,256]{1,0:T(8,128)(2,1)} %get-tuple-element.10), channel_id=1, source_target_pairs={{0,16},{16,32},{32,48},{48,64},{64,80},{80,96},{96,112},{112,128},... | collective-permute-start | bytes 589832 | tf_op jit(solution)/shard_map/ppermute | solution.py:15
  13.4 8.9 %collective-permute-start.1 = (bf16[384,256]{1,0:T(8,128)(2,1)}, bf16[384,256]{1,0:T(8,128)(2,1)}, u32[]{:S(2)}, u32[]{:S(2)}) collective-permute-start(bf16[384,256]{1,0:T(8,128)(2,1)} %collective-permute-done), channel_id=1, source_target_pairs={{0,1},{1,2},{2,3},{3,4},{4,5},{5,6},{6,7},{7,8},{8,9},{9,10},{10,1... | collective-permute-start | bytes 589832 | tf_op jit(solution)/shard_map/ppermute | solution.py:15
  22.4 7.5 %collective-permute-start.2 = (bf16[384,256]{1,0:T(8,128)(2,1)}, bf16[384,256]{1,0:T(8,128)(2,1)S(1)}, u32[]{:S(2)}, u32[]{:S(2)}) collective-permute-start(bf16[384,256]{1,0:T(8,128)(2,1)} %collective-permute-done.1), channel_id=1, source_target_pairs={{0,1},{1,2},{2,3},{3,4},{4,5},{5,6},{6,7},{7,8},{8,9},{9,10},{10,1... | collective-permute-start | bytes 589832 | tf_op jit(solution)/shard_map/ppermute | solution.py:15
  29.9 16.4 %copy-start.1 = (bf16[1920,256]{1,0:T(8,128)(2,1)}, bf16[1920,256]{1,0:T(8,128)(2,1)S(1)}, u32[]{:S(2)}) copy-start(bf16[1920,256]{1,0:T(8,128)(2,1)S(1)} %constant_dynamic-update-slice_fusion.2) | copy-start | bytes 2949124
  33.5 7.8 %copy-start = (f32[1920,384,8]{1,0,2:T(8,128)}, f32[1920,384,8]{1,0,2:T(8,128)S(1)}, u32[]{:S(2)}) copy-start(f32[1920,384,8]{1,0,2:T(8,128)S(1)} %get-tuple-element.20) | copy-start | bytes 70778880
  57.4 10.9 %copy-start.2 = (bf16[1920,256]{1,0:T(8,128)(2,1)S(1)}, bf16[1920,256]{1,0:T(8,128)(2,1)}, u32[]{:S(2)}) copy-start(bf16[1920,256]{1,0:T(8,128)(2,1)} %copy-done.1) | copy-start | bytes 2949124
  85.1 36.0 %slice-start = ((s8[11796480]{0:T(1024)(128)(4,1)}), s8[4194304]{0:T(1024)(128)(4,1)S(1)}, s32[]{:S(2)}) async-start(s8[11796480]{0:T(1024)(128)(4,1)} %bitcast.51), calls=%async_computation | async-start | bytes 8388608
  85.1 36.0 %slice-start.1 = ((s8[11796480]{0:T(1024)(128)(4,1)}), s8[4194304]{0:T(1024)(128)(4,1)S(1)}, s32[]{:S(2)}) async-start(s8[11796480]{0:T(1024)(128)(4,1)} %bitcast.51), calls=%async_computation.1 | async-start | bytes 8388608
  93.4 27.7 %slice-start.2 = ((s8[11796480]{0:T(1024)(128)(4,1)}), s8[3407872]{0:T(1024)(128)(4,1)S(1)}, s32[]{:S(2)}) async-start(s8[11796480]{0:T(1024)(128)(4,1)} %bitcast.51), calls=%async_computation.2 | async-start | bytes 6815744
  93.5 10.7 %collective-permute-start.4 = (f32[384,256]{0,1:T(8,128)S(1)}, f32[384,256]{0,1:T(8,128)S(1)}, u32[]{:S(2)}, u32[]{:S(2)}) collective-permute-start(f32[384,256]{0,1:T(8,128)S(1)} %fusion.10), channel_id=1, source_target_pairs={{0,15},{1,0},{2,1},{3,2},{4,3},{5,4},{6,5},{7,6},{8,7},{9,8},{10,9... | collective-permute-start | bytes 1179656 | tf_op jit(solution)/shard_map/ppermute | solution.py:15
  104.2 10.5 %collective-permute-start.5 = (f32[384,256]{0,1:T(8,128)S(1)}, f32[384,256]{0,1:T(8,128)S(1)}, u32[]{:S(2)}, u32[]{:S(2)}) collective-permute-start(f32[384,256]{0,1:T(8,128)S(1)} %fusion.12), channel_id=1, source_target_pairs={{0,15},{1,0},{2,1},{3,2},{4,3},{5,4},{6,5},{7,6},{8,7},{9,8},{10,9... | collective-permute-start | bytes 1179656 | tf_op jit(solution)/shard_map/ppermute | solution.py:15
  114.9 10.7 %collective-permute-start.7 = (f32[384,256]{0,1:T(8,128)S(1)}, f32[384,256]{0,1:T(8,128)}, u32[]{:S(2)}, u32[]{:S(2)}) collective-permute-start(f32[384,256]{0,1:T(8,128)S(1)} %get-tuple-element.7), channel_id=1, source_target_pairs={{0,240},{16,0},{32,16},{48,32},{64,48},{80,64},{96,80},{112,96},{1... | collective-permute-start | bytes 1179656 | tf_op jit(solution)/shard_map/ppermute | solution.py:15
  121.1 14.4 %collective-permute-start.6 = (f32[384,256]{0,1:T(8,128)S(1)}, f32[384,256]{0,1:T(8,128)}, u32[]{:S(2)}, u32[]{:S(2)}) collective-permute-start(f32[384,256]{0,1:T(8,128)S(1)} %get-tuple-element.6), channel_id=1, source_target_pairs={{0,15},{1,0},{2,1},{3,2},{4,3},{5,4},{6,5},{7,6},{8,7},{9,8},{10,9... | collective-permute-start | bytes 1179656 | tf_op jit(solution)/shard_map/ppermute | solution.py:15
where the time goes:
time: 140 us; the launch traced here: 138 us
  matrix products  52.4 us (37%)
  waiting for transfers between devices  36.4 us (26%)
  starting transfers between devices  21 us (15%)
  local copies, waits for them, and re-layouts  19 us (14%)
  other arithmetic  8.58 us (6%)
    ppermute x8, waiting for transfers between devices, shifted(): lax.ppermute(value, axis, [(i, (i + by) % size) for i in range(size)])  36.4 us
    ppermute x8, starting transfers between devices, shifted(): lax.ppermute(value, axis, [(i, (i + by) % size) for i in range(size)])  21 us
    dot_general x1, matrix products, window_attention(): jnp.einsum('thd,kd->htk', grad_heads, value_part, preferred_element_type=...  16.8 us
    unnamed x24, local copies, waits for them, and re-layouts  15.5 us
    dot_general x1, matrix products, window_attention(): jnp.einsum('htk,kd->thd', prob_round, value_part, preferred_element_type=...  10.9 us
    dot_general x1, matrix products, window_attention(): jnp.einsum('htk,thd->kd', prob_round, grad_heads, preferred_element_type=...  10.8 us
    dot_general x1, matrix products, window_attention(): jnp.einsum('htk,thd->kd', score_round, query_heads, preferred_element_typ...  8.31 us
    reduce_sum x1, other arithmetic, window_attention(): jnp.sum(jnp.exp(scores - row_max), axis=2, keepdims=True)  4.89 us
  transfers between devices with their start and end apart: 8, of which 6 were waited for; matrix products, arithmetic and copies ran while one was open for 8% of the time, Pallas kernels for 0%

commit v1 on v0

v1 whole, which is shorter than its diff:
```python
import functools
import math

import jax
import jax.numpy as jnp
from jax import lax
from jax.experimental import pallas as pl
from jax.experimental.pallas import tpu as pltpu
from jax.sharding import PartitionSpec as P

HEADS = 8
HEAD = 128
STEPS = 4
BLOCKS = STEPS + 1
PAIRS = HEADS // 2
ROOT = 1.0 / math.sqrt(HEAD)
SCALE = ROOT * math.log2(math.e)
BIG = 1e30
SAFE = 60.0
TILE = 256
UNROLL = 4
F32 = jnp.float32
BF16 = jnp.bfloat16
VMEM = pl.BlockSpec(memory_space=pltpu.VMEM)
SMEM = pl.BlockSpec(memory_space=pltpu.SMEM)


def fold(value, op):
    rows, lanes = value.shape
    return op(value.reshape(rows // 8, 8, lanes), axis=0)


def heads_of(ref, pair):
    first = pl.multiple_of(pair * 2 * HEAD, HEAD)
    second = pl.multiple_of(first + HEAD, HEAD)
    return jnp.concatenate([ref[:, pl.ds(first, HEAD)], ref[:, pl.ds(second, HEAD)]], axis=0)


def turn(q_ref, go_ref, qs_ref, gs_ref, qt_ref, gt_ref, norm_ref):
    norm = jnp.zeros((8, 2 * q_ref.shape[0]), F32)
    for pair in range(PAIRS):
        qs_ref[pair] = heads_of(q_ref, pair)
        gs_ref[pair] = heads_of(go_ref, pair)
        turned = qs_ref[pair].T
        qt_ref[pair] = turned
        gt_ref[pair] = gs_ref[pair].T
        square = turned.astype(F32)
        norm = jnp.maximum(norm, jnp.sum(fold(square * square, jnp.sum), axis=0, keepdims=True))
    norm_ref[...] = norm


def again_kernel(spans_ref, own_ref, out_ref):
    out_ref[...] = own_ref[...]


def small(norm_ref, kv_refs):
    longest = jnp.zeros((kv_refs[0].shape[0], 1), F32)
    for ref in kv_refs:
        key = ref[:, :HEAD].astype(F32)
        longest = jnp.maximum(longest, jnp.sum(key * key, axis=1, keepdims=True))
    return jnp.max(longest) * jnp.max(norm_ref[...]) * (SCALE * SCALE) < SAFE * SAFE


def either(safe, make):
    @pl.when(safe)
    def _():
        make(False)

    @pl.when(jnp.logical_not(safe))
    def _():
        make(True)


def scores(exact, pair, spans_ref, numbers, qt_ref, gt_ref, kv_refs, prob, gprob, mask):
    tok = kv_refs[0].shape[0]
    span = tok // 2
    wide = 2 * tok
    found = {}
    for t in range(wide // TILE):
        cols = slice(t * TILE, (t + 1) * TILE)
        lane = lax.broadcasted_iota(jnp.int32, (1, TILE), 1) + t * TILE
        qpos = jnp.where((lane % tok) < span, spans_ref[0], spans_ref[1])
        for b, number in enumerate(numbers):
            s = jnp.dot(kv_refs[b][:, :HEAD], qt_ref[pair, :, cols], preferred_element_type=F32)
            g = jnp.dot(kv_refs[b][:, HEAD:], gt_ref[pair, :, cols], preferred_element_type=F32)
            if b == 0 and mask is not None:
                s = s + mask[:, cols]
            bias = [jnp.where(qpos >= spans_ref[2 * number + half], 0.0, BIG) for half in range(2)]
            top = jnp.zeros((1, TILE), F32)
            if exact:
                top = jnp.maximum(fold(s[:span], jnp.max) - bias[0], fold(s[span:], jnp.max) - bias[1])
                top = jnp.max(top, axis=0, keepdims=True) * SCALE
            total = jnp.zeros((8, TILE), F32)
            dots = jnp.zeros((8, TILE), F32)
            for half in range(2):
                part = slice(half * span, (half + 1) * span)
                rows = slice(b * tok + half * span, b * tok + (half + 1) * span)
                e = jnp.exp2(s[part] * SCALE - (top + bias[half]))
                total = total + fold(e, jnp.sum)
                dots = dots + fold(e * g[part], jnp.sum)
                prob[pair, rows, cols] = e.astype(BF16)
                gprob[pair, rows, cols] = g[part].astype(BF16)
            found[t, b] = (top, jnp.sum(total, axis=0, keepdims=True), jnp.sum(dots, axis=0, keepdims=True))
    return [
        [jnp.concatenate([found[t, b][n] for t in range(wide // TILE)], axis=1) for n in range(3)]
        for b in range(len(numbers))
    ]


def keep(ref, pair, rows):
    for n, row in enumerate(rows):
        ref[pair, n : n + 1, :] = row


def diagonal(mask):
    tok, wide = mask.shape
    key = lax.broadcasted_iota(jnp.int32, (tok, wide), 0)
    query = lax.broadcasted_iota(jnp.int32, (tok, wide), 1)
    query = jnp.where(query >= tok, query - tok, query)
    same = (key >= tok // 2) == (query >= tok // 2)
    mask[...] = jnp.where(same & (key > query), -BIG, 0.0)


def merged(found):
    best = functools.reduce(jnp.maximum, [top for top, _, _ in found])
    weights = [jnp.exp2(top - best) for top, _, _ in found]
    total = sum(w * x for w, (_, x, _) in zip(weights, found))
    product = sum(w * x for w, (_, _, x) in zip(weights, found))
    return best, total, product, weights


def scores_kernel(numbers, spans_ref, *refs):
    count = len(numbers)
    mask = before = None
    if numbers[0] == 0:
        q_ref, go_ref, kv_ref, qs_ref, gs_ref, qt_ref, gt_ref, norm_ref, prob, gprob, stats, mask = refs
        kv_refs = [kv_ref]
        turn(q_ref, go_ref, qs_ref, gs_ref, qt_ref, gt_ref, norm_ref)
        diagonal(mask)
    else:
        qt_ref, gt_ref, norm_ref = refs[:3]
        kv_refs, (before, prob, gprob, stats) = refs[3 : 3 + count], refs[3 + count :]

    def make(exact):
        def step(pair, carry):
            found = scores(exact, pair, spans_ref, numbers, qt_ref, gt_ref, kv_refs, prob, gprob, mask)
            if before is None:
                keep(stats, pair, found[0])
            else:
                best, total, product, weights = merged([[before[pair, n : n + 1, :] for n in range(3)]] + found)
                keep(stats, pair, [best, total, product] + weights)
            return carry

        lax.fori_loop(0, PAIRS, step, 0, unroll=1 if exact else UNROLL)

    either(small(norm_ref, kv_refs), make)


def grads(pair, q_ref, go_ref, rates, rowdot, prob, gprob, dscore, dk, dv):
    tok = q_ref.shape[1] // 2
    q, go = q_ref[pair], go_ref[pair]
    for b, rate in enumerate(rates):
        rows = slice(b * tok, (b + 1) * tok)
        p = prob[pair, rows, :].astype(F32) * rate
        ds = (p * (gprob[pair, rows, :].astype(F32) - rowdot)).astype(BF16)
        dscore[pair, rows, :] = ds
        dk[rows, :] += jnp.dot(ds, q, preferred_element_type=F32)
        dv[rows, :] += jnp.dot(p.astype(BF16), go, preferred_element_type=F32)


def finish(dk, dv, outs):
    for b, out in enumerate(outs):
        tok = out.shape[0]
        out[:, :HEAD] = (dk[b * tok : (b + 1) * tok, :] * ROOT).astype(out.dtype)
        out[:, HEAD:] = dv[b * tok : (b + 1) * tok, :].astype(out.dtype)


def last_kernel(
    spans_ref, q_ref, go_ref, qt_ref, gt_ref, norm_ref, stats, kv_ref, rates, dscore, dkv, prob, gprob
):
    def make(exact):
        def find(pair, carry):
            (found,) = scores(exact, pair, spans_ref, [BLOCKS - 1], qt_ref, gt_ref, [kv_ref], prob, gprob, None)
            _, total, product, weights = merged([[stats[pair, n : n + 1, :] for n in range(3)], found])
            inv = 1.0 / total
            keep(rates, pair, [weights[0] * inv, product * inv, weights[1] * inv])
            return carry

        lax.fori_loop(0, PAIRS, find, 0, unroll=1 if exact else UNROLL)

    either(small(norm_ref, [kv_ref]), make)
    dk = dv = 0.0
    for pair in range(PAIRS):
        rowdot, rate = rates[pair, 1:2, :], rates[pair, 2:3, :]
        p = prob[pair].astype(F32) * rate
        ds = (p * (gprob[pair].astype(F32) - rowdot)).astype(BF16)
        p = p.astype(BF16)
        dscore[pair] = ds
        dk = dk + jnp.dot(ds, q_ref[pair], preferred_element_type=F32)
        dv = dv + jnp.dot(p, go_ref[pair], preferred_element_type=F32)

    dkv[:, :HEAD] = (dk * ROOT).astype(BF16)
    dkv[:, HEAD:] = dv.astype(BF16)


def grads_kernel(chains, q_ref, go_ref, rates, *refs):
    stats, (prob, gprob, dscore), outs, (dk, dv) = refs[:2], refs[2:5], refs[5:-2], refs[-2:]
    dk[...] = jnp.zeros_like(dk)
    dv[...] = jnp.zeros_like(dv)

    def step(pair, carry):
        each = []
        for chain in chains:
            rate = rates[pair, 0:1, :]
            for which, row in chain:
                rate = rate * stats[which][pair, row : row + 1, :]
            each.append(rate)
        grads(pair, q_ref, go_ref, each, rates[pair, 1:2, :], prob, gprob, dscore, dk, dv)
        return carry

    lax.fori_loop(0, PAIRS, step, 0, unroll=UNROLL)
    finish(dk, dv, outs)


def own_kernel(q_ref, go_ref, rates, near, far, prob, gprob, ds_first, ds_two, ds_last, *refs):
    kv_refs, (dq_ref, dkv, kt, dscore, dk, dv) = refs[:BLOCKS], refs[BLOCKS:]
    tok = dkv.shape[0]
    dk[...] = jnp.zeros_like(dk)
    dv[...] = jnp.zeros_like(dv)
    for b, ref in enumerate(kv_refs):
        kt[:, b * tok : (b + 1) * tok] = ref[:, :HEAD].T

    def step(pair, carry):
        rate = near[pair, 3:4, :] * far[pair, 3:4, :] * rates[pair, 0:1, :]
        grads(pair, q_ref, go_ref, [rate], rates[pair, 1:2, :], prob, gprob, dscore, dk, dv)
        dqt, start = 0.0, 0
        for part in (dscore, ds_first, ds_two, ds_last):
            end = start + part.shape[1]
            dqt = dqt + jnp.dot(kt[:, start:end], part[pair], preferred_element_type=F32)
            start = end
        dq = (dqt * ROOT).T.astype(BF16)
        first = pl.multiple_of(pair * 2 * HEAD, HEAD)
        second = pl.multiple_of(first + HEAD, HEAD)
        dq_ref[:, pl.ds(first, HEAD)] = dq[:tok]
        dq_ref[:, pl.ds(second, HEAD)] = dq[tok:]
        return carry

    lax.fori_loop(0, PAIRS, step, 0, unroll=UNROLL)
    finish(dk, dv, [dkv])


def shape(dtype, *sizes):
    return jax.ShapeDtypeStruct(sizes, dtype)


def call(kernel, name, operands, outs, scratch, flops):
    return pl.pallas_call(
        kernel,
        name=name,
        out_shape=outs,
        in_specs=[SMEM if x.dtype == jnp.int32 else VMEM for x in operands],
        out_specs=[VMEM] * len(outs),
        scratch_shapes=scratch,
        cost_estimate=pl.CostEstimate(flops=flops, bytes_accessed=0, transcendentals=0),
        compiler_params=pltpu.CompilerParams(vmem_limit_bytes=14 * 2**20),
    )(*operands)


def work(tok, blocks, products):
    return 4 * blocks * products * tok * tok * HEADS * HEAD


def again(spans, kv):
    return call(again_kernel, "again", [spans, kv], [shape(BF16, *kv.shape)], [], 0)[0]


def own_scores(spans, queries, grad_out, kv):
    tok = kv.shape[0]
    wide = 2 * tok
    return call(
        functools.partial(scores_kernel, [0]),
        "own_scores",
        [spans, queries, grad_out, kv],
        [shape(BF16, PAIRS, wide, HEAD)] * 2
        + [shape(BF16, PAIRS, HEAD, wide)] * 2
        + [shape(F32, 8, wide)]
        + [shape(BF16, PAIRS, tok, wide)] * 2
        + [shape(F32, PAIRS, 8, wide)],
        [pltpu.VMEM((tok, wide), F32)],
        work(tok, 1, 2),
    )


def score(name, spans, qt, gt, norm, blocks, numbers, *before):
    tok = blocks[0].shape[0]
    keys, wide = len(blocks) * tok, 2 * tok
    return call(
        functools.partial(scores_kernel, numbers),
        name,
        [spans, qt, gt, norm, *blocks, *before],
        [shape(BF16, PAIRS, keys, wide), shape(BF16, PAIRS, keys, wide), shape(F32, PAIRS, 8, wide)],
        [],
        work(tok, len(blocks), 2),
    )


def last(spans, queries, grad_out, qt, gt, norm, stats, kv):
    tok = queries.shape[1] // 2
    wide = 2 * tok
    return call(
        last_kernel,
        "last_block",
        [spans, queries, grad_out, qt, gt, norm, stats, kv],
        [shape(F32, PAIRS, 8, wide), shape(BF16, PAIRS, tok, wide), shape(BF16, tok, 2 * HEAD)],
        [pltpu.VMEM((PAIRS, tok, wide), BF16)] * 2,
        work(tok, 1, 4),
    )


def block_grads(name, queries, grad_out, rates, near, far, prob, gprob, chains):
    tok = queries.shape[1] // 2
    keys, wide = prob.shape[1:]
    count = keys // tok
    return call(
        functools.partial(grads_kernel, chains),
        name,
        [queries, grad_out, rates, near, far, prob, gprob],
        [shape(BF16, PAIRS, keys, wide)] + [shape(BF16, tok, 2 * HEAD)] * count,
        [pltpu.VMEM((keys, HEAD), F32)] * 2,
        work(tok, count, 2),
    )


def own_grads(queries, grad_out, rates, near, far, prob, gprob, dscores, blocks):
    tok = queries.shape[1] // 2
    return call(
        own_kernel,
        "own_grads",
        [queries, grad_out, rates, near, far, prob, gprob, *dscores, *blocks],
        [shape(BF16, tok, HEADS * HEAD), shape(F32, tok, 2 * HEAD)],
        [
            pltpu.VMEM((HEAD, BLOCKS * tok), BF16),
            pltpu.VMEM((PAIRS, tok, 2 * tok), BF16),
            pltpu.VMEM((tok, HEAD), F32),
            pltpu.VMEM((tok, HEAD), F32),
        ],
        work(tok, BLOCKS, 2),
    )


def rotate(value, axis, by):
    size = lax.axis_size(axis)
    return lax.ppermute(value, axis, [(i, (i + by) % size) for i in range(size)])


def body(queries, keys, values, grad_out, span_order):
    inner_count = lax.axis_size("inner")
    outer_count = lax.axis_size("outer")
    outer_index = lax.axis_index("outer")
    inner_index = lax.axis_index("inner")
    left = lax.broadcasted_iota(jnp.int32, (keys.shape[0], 2 * HEAD), 1) < HEAD
    zero = jnp.zeros((), BF16)
    own = jnp.where(
        left, lax.pad(keys, zero, ((0, 0, 0), (0, HEAD, 0))), lax.pad(values, zero, ((0, 0, 0), (HEAD, 0, 0)))
    )
    first = rotate(own, "inner", 1)
    numbers = [outer_index * inner_count + (inner_index - stride) % inner_count for stride in range(STEPS)]
    numbers.insert(3, (outer_index - 1) % outer_count * inner_count + inner_index)
    spans = jnp.concatenate([lax.dynamic_slice_in_dim(span_order, 2 * n, 2, 0) for n in numbers])
    later = again(spans, own)
    second = rotate(later, "inner", 2)
    outer = rotate(later, "outer", 1)
    third = rotate(first, "inner", 2)

    queries, grad_out, *turns, e0, g0, s0 = own_scores(spans, queries, grad_out, own)
    e1, g1, near = score("first_scores", spans, *turns, [first], [1], s0)
    e2, g2, far = score("two_scores", spans, *turns, [second, outer], [2, 3], near)
    rates, ds3, p_third = last(spans, queries, grad_out, *turns, far, third)
    third_back = rotate(p_third, "inner", -2)
    stats = (rates, near, far)
    ds2, p_second, p_outer = block_grads("two_grads", queries, grad_out, *stats, e2, g2, [[(1, 4)], [(1, 5)]])
    second_back = rotate(p_second, "inner", -2)
    outer_back = rotate(p_outer, "outer", -1)
    ds1, p_first = block_grads("first_grads", queries, grad_out, *stats, e1, g1, [[(0, 4), (1, 3)]])
    chain = (p_first.astype(F32) + third_back.astype(F32)).astype(BF16)
    chain_back = rotate(chain, "inner", -1)
    blocks = [own, first, second, outer, third]
    grad_q, p_own = own_grads(queries, grad_out, *stats, e0, g0, [ds1, ds2, ds3], blocks)
    summed = p_own + chain_back.astype(F32) + second_back.astype(F32) + outer_back.astype(F32)
    return (grad_q, summed[:, :HEAD].astype(BF16), summed[:, HEAD:].astype(BF16))


def solution(mesh):
    rows = P(("outer", "inner"), None)
    return jax.shard_map(
        body,
        mesh=mesh,
        in_specs=(rows, rows, rows, rows, P()),
        out_specs=(rows, rows, rows),
        check_vma=False,
    )
```

time: 140 us -> 50.2 us (0.36); the launches traced: 138 us -> 50 us
  matrix products: 52.4 us -> 0 us
  waiting for transfers between devices: 36.4 us -> 5.76 us
  Pallas kernels: 0 us -> 23.6 us
  local copies, waits for them, and re-layouts: 19 us -> 3.98 us
  other arithmetic: 8.58 us -> 1.14 us
  starting transfers between devices: 21 us -> 14.8 us
    dot_general x6 -> x0, matrix products: 52.4 us -> none  [the longest x1 16.8 us: window_attention(): jnp.einsum('thd,kd->htk', grad_heads, value_part, preferred_element_type=...]
    ppermute x8, waiting for transfers between devices: 36.4 us -> 5.76 us  [rotate(): lax.ppermute(value, axis, [(i, (i + by) % size) for i in range(size)])]
    pallas_call x0 -> x8, Pallas kernels: none -> 23.6 us  [call(): pl.pallas_call(kernel, name=name, out_shape=outs, in_specs=[SMEM if x.dty...]
    unnamed x24 -> x4, local copies, waits for them, and re-layouts: 15.5 us -> 2.27 us
    ppermute x8, starting transfers between devices: 21 us -> 14.8 us  [rotate(): lax.ppermute(value, axis, [(i, (i + by) % size) for i in range(size)])]
    reduce_sum x2 -> x0, other arithmetic: 5.12 us -> none  [the longest x1 4.89 us: window_attention(): jnp.sum(jnp.exp(scores - row_max), axis=2, keepdims=True)]
    concatenate x3 -> x1, local copies, waits for them, and re-layouts: 1.58 us -> 0.08 us  [body(): jnp.concatenate([lax.dynamic_slice_in_dim(span_order, 2 * n, 2, 0) for n...]
    reshape x1 -> x0, local copies, waits for them, and re-layouts: 1.49 us -> none  [window_attention(): query_heads = query_rows.reshape(tok_rows, HEADS, HEAD)]
  transfers between devices with their start and end apart: 8 -> 8, of which waited for: 6 -> 2; matrix products, arithmetic and copies ran while one was open for 8% -> 2% of each run, Pallas kernels for 0% -> 38%
where the time goes in v1:
time: 50.2 us; the launch traced here: 50 us
  Pallas kernels  23.6 us (47%)
  starting transfers between devices  14.8 us (29%)
  waiting for transfers between devices  5.76 us (11%)
  local copies, waits for them, and re-layouts  3.98 us (8%)
  other arithmetic  1.14 us (2%)
  between operations  0.74 us (1%)
    pallas_call x8, Pallas kernels, call(): pl.pallas_call(kernel, name=name, out_shape=outs, in_specs=[SMEM if x.dty...  23.6 us
    ppermute x8, starting transfers between devices, rotate(): lax.ppermute(value, axis, [(i, (i + by) % size) for i in range(size)])  14.8 us
    ppermute x8, waiting for transfers between devices, rotate(): lax.ppermute(value, axis, [(i, (i + by) % size) for i in range(size)])  5.76 us
    unnamed x4, local copies, waits for them, and re-layouts  2.27 us
  transfers between devices with their start and end apart: 8, of which 2 were waited for; matrix products, arithmetic and copies ran while one was open for 2% of the time, Pallas kernels for 38%

profile of v1, /device:TPU:123, one launch (start us, length us, event | category | flops | bytes accessed | tf_op | source)
XLA Modules:
  0.0 50.0 jit_solution(11867423843153237036)
XLA Ops:
  0.6 1.0 %pad_select_fusion.refs_2_.own_ref.refs_0_ = bf16[384,256]{1,0:T(8,128)(2,1)S(1)} fusion(bf16[384,128]{1,0:T(8,128)(2,1)} %param.7, bf16[384,128]{1,0:T(8,128)(2,1)} %param.6, pred[256]{0:T(512)(128)(4,1)S(1)} %iota_compare_fusion), kind=kLoop, calls=%fused_computation.2 | loop fusion | flops 98304 | bytes 393472 | tf_op jit(solution)/shard_map/jit(_where)/select_n | solution.py:363
  1.6 3.6 %collective-permute-start.2 = (bf16[384,256]{1,0:T(8,128)(2,1)S(1)}, bf16[384,256]{1,0:T(8,128)(2,1)S(1)}, u32[]{:S(2)}, u32[]{:S(2)}) collective-permute-start(bf16[384,256]{1,0:T(8,128)(2,1)S(1)} %pad_select_fusion.refs_2_.own_ref.refs_0_), channel_id=1, source_target_pairs={{0,1},{1,2},{2,3},{3,4},{4,5},{5,6},{6,7},{7,8},{8,9},{9,10},{10,1... | collective-permute-start | bytes 589832 | tf_op jit(solution)/shard_map/ppermute | solution.py:353
  5.2 0.9 %fusion.1 = (s32[2]{0:T(128)S(1)}, s32[2]{0:T(128)S(1)}, s32[2]{0:T(128)S(1)}, s32[2]{0:T(128)S(1)}, s32[2]{0:T(128)S(1)}) fusion(s32[512]{0:T(512)} %param.9, s32[]{:T(128)S(6)} %select_n.51, s32[]{:T(128)S(6)} %select_n.47, s32[]{:T(128)S(6)} %select_n.45, s32[]{:T(128)S(6)} %select_n.43, s32[]{:T(128)S(6)} %select_n.49), kind=kLoop, calls=%fused_computation.5 | loop fusion | bytes 100 | tf_op jit(solution)/shard_map/dynamic_slice | solution.py:369
  6.2 0.1 concatenate.3.spans_ref
  6.2 0.6 %again.1 = bf16[384,256]{1,0:T(8,128)(2,1)S(1)} custom-call(s32[10]{0:T(128)S(1)} %concatenate.3.spans_ref, bf16[384,256]{1,0:T(8,128)(2,1)S(1)} %pad_select_fusion.refs_2_.own_ref.refs_0_), custom_call_target="tpu_custom_call" | custom-call | tf_op jit(solution)/shard_map/again/pallas_call | solution.py:257
  6.8 0.8 %collective-permute-start = (bf16[384,256]{1,0:T(8,128)(2,1)S(1)}, bf16[384,256]{1,0:T(8,128)(2,1)S(1)}, u32[]{:S(2)}, u32[]{:S(2)}) collective-permute-start(bf16[384,256]{1,0:T(8,128)(2,1)S(1)} %again.1), channel_id=1, source_target_pairs={{0,2},{1,3},{2,4},{3,5},{4,6},{5,7},{6,8},{7,9},{8,10},{9,11},{10,... | collective-permute-start | bytes 589832 | tf_op jit(solution)/shard_map/ppermute | solution.py:353
  7.6 1.6 %collective-permute-start.1 = (bf16[384,256]{1,0:T(8,128)(2,1)S(1)}, bf16[384,256]{1,0:T(8,128)(2,1)S(1)}, u32[]{:S(2)}, u32[]{:S(2)}) collective-permute-start(bf16[384,256]{1,0:T(8,128)(2,1)S(1)} %again.1), channel_id=1, source_target_pairs={{0,16},{16,32},{32,48},{48,64},{64,80},{80,96},{96,112},{112,128},... | collective-permute-start | bytes 589832 | tf_op jit(solution)/shard_map/ppermute | solution.py:353
  9.2 0.0 copy-start
  9.2 1.1 %copy-done = bf16[384,1024]{1,0:T(8,128)(2,1)S(1)} copy-done((bf16[384,1024]{1,0:T(8,128)(2,1)S(1)}, bf16[384,1024]{1,0:T(8,128)(2,1)}, u32[]{:S(2)}) %copy-start) | copy-done | bytes 786456
  10.4 0.0 copy-start.1
  10.4 1.1 %copy-done.1 = bf16[384,1024]{1,0:T(8,128)(2,1)S(1)} copy-done((bf16[384,1024]{1,0:T(8,128)(2,1)S(1)}, bf16[384,1024]{1,0:T(8,128)(2,1)}, u32[]{:S(2)}) %copy-start.1) | copy-done | bytes 786456
  11.5 2.8 %own_scores.1 = (bf16[4,768,128]{2,1,0:T(8,128)(2,1)S(1)}, bf16[4,768,128]{2,1,0:T(8,128)(2,1)S(1)}, bf16[4,128,768]{2,1,0:T(8,128)(2,1)S(1)}, bf16[4,128,768]{2...) custom-call(s32[10]{0:T(128)S(1)} %concatenate.3.spans_ref, ...), custom_call_target="tpu_custom_call" | custom-call | flops 1207959552 | tf_op jit(solution)/shard_map/own_scores/pallas_call | solution.py:257
  14.3 0.0 collective-permute-done.2.refs_3_.refs_1_
  14.3 0.8 %collective-permute-start.3 = (bf16[384,256]{1,0:T(8,128)(2,1)S(1)}, bf16[384,256]{1,0:T(8,128)(2,1)S(1)}, u32[]{:S(2)}, u32[]{:S(2)}) collective-permute-start(bf16[384,256]{1,0:T(8,128)(2,1)S(1)} %collective-permute-done.2.refs_3_.refs_1_), channel_id=1, source_target_pairs={{0,2},{1,3},{2,4},{3,5},{4,6},{5,7},{6,8},{7,9},{8,10},{9,11},{10,... | collective-permute-start | bytes 589832 | tf_op jit(solution)/shard_map/ppermute | solution.py:353
  15.2 3.4 %first_scores.1 = (bf16[4,384,768]{2,1,0:T(8,128)(2,1)S(1)}, bf16[4,384,768]{2,1,0:T(8,128)(2,1)S(1)}, f32[4,8,768]{2,1,0:T(8,128)S(1)}) custom-call(s32[10]{0:T(128)S(1)} %concatenate.3.spans_ref, bf16[4,128,768]{2,1,0:T(8,128)(2,1)S(1)} %get-tuple-element.29.refs_0_.qt_ref, bf16[4,128,768]{2,1,0:T(8,128)(2,1)S(1)} %get-tuple-element.30.refs_1_.gt_ref, ...), custom_call_target="tpu_custom_call" | custom-call | flops 1207959552 | tf_op jit(solution)/shard_map/first_scores/pallas_call | solution.py:257
  18.5 0.0 collective-permute-done.refs_3_.refs_2_
  18.6 0.0 collective-permute-done.1.refs_4_.refs_3_
  18.6 3.6 %two_scores.1 = (bf16[4,768,768]{2,1,0:T(8,128)(2,1)S(1)}, bf16[4,768,768]{2,1,0:T(8,128)(2,1)S(1)}, f32[4,8,768]{2,1,0:T(8,128)S(1)}) custom-call(s32[10]{0:T(128)S(1)} %concatenate.3.spans_ref, bf16[4,128,768]{2,1,0:T(8,128)(2,1)S(1)} %get-tuple-element.29.refs_0_.qt_ref, bf16[4,128,768]{2,1,0:T(8,128)(2,1)S(1)} %get-tuple-element.30.refs_1_.gt_ref, ...), custom_call_target="tpu_custom_call" | custom-call | flops 2415919104 | tf_op jit(solution)/shard_map/two_scores/pallas_call | solution.py:257
  22.2 0.0 collective-permute-done.3.kv_ref.refs_4_
  22.2 4.8 %last_block.1 = (f32[4,8,768]{2,1,0:T(8,128)S(1)}, bf16[4,384,768]{2,1,0:T(8,128)(2,1)S(1)}, bf16[384,256]{1,0:T(8,128)(2,1)S(1)}) custom-call(s32[10]{0:T(128)S(1)} %concatenate.3.spans_ref, bf16[4,768,128]{2,1,0:T(8,128)(2,1)S(1)} %get-tuple-element.27.q_ref, bf16[4,768,128]{2,1,0:T(8,128)(2,1)S(1)} %get-tuple-element.28.go_ref, ...), custom_call_target="tpu_custom_call" | custom-call | flops 2415919104 | tf_op jit(solution)/shard_map/last_block/pallas_call | solution.py:257
  27.0 0.8 %collective-permute-start.4 = (bf16[384,256]{1,0:T(8,128)(2,1)S(1)}, bf16[384,256]{1,0:T(8,128)(2,1)S(1)}, u32[]{:S(2)}, u32[]{:S(2)}) collective-permute-start(bf16[384,256]{1,0:T(8,128)(2,1)S(1)} %get-tuple-element.48), channel_id=1, source_target_pairs={{0,14},{1,15},{2,0},{3,1},{4,2},{5,3},{6,4},{7,5},{8,6},{9,7},{10,... | collective-permute-start | bytes 589832 | tf_op jit(solution)/shard_map/ppermute | solution.py:353
  27.8 2.8 %two_grads.1 = (bf16[4,768,768]{2,1,0:T(8,128)(2,1)S(1)}, bf16[384,256]{1,0:T(8,128)(2,1)S(1)}, bf16[384,256]{1,0:T(8,128)(2,1)S(1)}) custom-call(bf16[4,768,128]{2,1,0:T(8,128)(2,1)S(1)} %get-tuple-element.27.q_ref, bf16[4,768,128]{2,1,0:T(8,128)(2,1)S(1)} %get-tuple-element.28.go_ref, f32[4,8,768]{2,1,0:T(8,128)S(1)} %get-tuple-element.35.rates, ...), custom_call_target="tpu_custom_call" | custom-call | flops 2415919104 | tf_op jit(solution)/shard_map/two_grads/pallas_call | solution.py:257
  30.6 0.1 collective-permute-start.6
  30.6 0.3 collective-permute-start.7
  30.9 1.4 %first_grads.1 = (bf16[4,384,768]{2,1,0:T(8,128)(2,1)S(1)}, bf16[384,256]{1,0:T(8,128)(2,1)S(1)}) custom-call(bf16[4,768,128]{2,1,0:T(8,128)(2,1)S(1)} %get-tuple-element.27.q_ref, bf16[4,768,128]{2,1,0:T(8,128)(2,1)S(1)} %get-tuple-element.28.go_ref, f32[4,8,768]{2,1,0:T(8,128)S(1)} %get-tuple-element.35.rates, ...), custom_call_target="tpu_custom_call" | custom-call | flops 1207959552 | tf_op jit(solution)/shard_map/first_grads/pallas_call | solution.py:257
  32.3 2.6 %collective-permute-done.4 = bf16[384,256]{1,0:T(8,128)(2,1)S(1)} collective-permute-done((bf16[384,256]{1,0:T(8,128)(2,1)S(1)}, bf16[384,256]{1,0:T(8,128)(2,1)S(1)}, u32[]{:S(2)}, u32[]{:S(2)}) %collective-permute-start.4) | collective-permute-done | bytes 196640 | tf_op jit(solution)/shard_map/ppermute | solution.py:353
  34.9 0.1 add_convert_fusion.1
  35.0 6.8 %collective-permute-start.5 = (bf16[384,256]{1,0:T(8,128)(2,1)S(1)}, bf16[384,256]{1,0:T(8,128)(2,1)S(1)}, u32[]{:S(2)}, u32[]{:S(2)}) collective-permute-start(bf16[384,256]{1,0:T(8,128)(2,1)S(1)} %add_convert_fusion.1), channel_id=1, source_target_pairs={{0,15},{1,0},{2,1},{3,2},{4,3},{5,4},{6,5},{7,6},{8,7},{9,8},{10,9... | collective-permute-start | bytes 589832 | tf_op jit(solution)/shard_map/ppermute | solution.py:353
  41.8 4.2 %own_grads.1 = (bf16[384,1024]{1,0:T(8,128)(2,1)}, f32[384,256]{1,0:T(8,128)S(1)}) custom-call(bf16[4,768,128]{2,1,0:T(8,128)(2,1)S(1)} %get-tuple-element.27.q_ref, bf16[4,768,128]{2,1,0:T(8,128)(2,1)S(1)} %get-tuple-element.28.go_ref, f32[4,8,768]{2,1,0:T(8,128)S(1)} %get-tuple-element.35.rates, f32[4,8,768]{2,1,0:T(8,128)S(1)} %get-tuple-element.33.refs_5_.refs_0_.near, ...), custom_call_target="tpu_custom_call" | custom-call | flops 6039797760 | tf_op jit(solution)/shard_map/own_grads/pallas_call | solution.py:257
  46.0 0.0 collective-permute-done.6
  46.0 0.0 collective-permute-done.7
  46.0 3.1 %collective-permute-done.5 = bf16[384,256]{1,0:T(8,128)(2,1)S(1)} collective-permute-done((bf16[384,256]{1,0:T(8,128)(2,1)S(1)}, bf16[384,256]{1,0:T(8,128)(2,1)S(1)}, u32[]{:S(2)}, u32[]{:S(2)}) %collective-permute-start.5) | collective-permute-done | bytes 196640 | tf_op jit(solution)/shard_map/ppermute | solution.py:353
  49.2 0.1 add_convert_fusion
  49.3 0.7 %fusion = (bf16[384,128]{1,0:T(8,128)(2,1)}, bf16[384,128]{1,0:T(8,128)(2,1)}) fusion(bf16[384,256]{1,0:T(8,128)(2,1)S(1)} %add_convert_fusion), kind=kLoop, calls=%fused_computation.4 | loop fusion | bytes 393216 | tf_op jit(solution)/shard_map/slice | solution.py:390
  (1 shorter events, 0.0 us)
Async XLA Ops:
  1.6 12.7 %collective-permute-start.2 = (bf16[384,256]{1,0:T(8,128)(2,1)S(1)}, bf16[384,256]{1,0:T(8,128)(2,1)S(1)}, u32[]{:S(2)}, u32[]{:S(2)}) collective-permute-start(bf16[384,256]{1,0:T(8,128)(2,1)S(1)} %pad_select_fusion.refs_2_.own_ref.refs_0_), channel_id=1, source_target_pairs={{0,1},{1,2},{2,3},{3,4},{4,5},{5,6},{6,7},{7,8},{8,9},{9,10},{10,1... | collective-permute-start | bytes 589832 | tf_op jit(solution)/shard_map/ppermute | solution.py:353
  6.8 11.7 %collective-permute-start = (bf16[384,256]{1,0:T(8,128)(2,1)S(1)}, bf16[384,256]{1,0:T(8,128)(2,1)S(1)}, u32[]{:S(2)}, u32[]{:S(2)}) collective-permute-start(bf16[384,256]{1,0:T(8,128)(2,1)S(1)} %again.1), channel_id=1, source_target_pairs={{0,2},{1,3},{2,4},{3,5},{4,6},{5,7},{6,8},{7,9},{8,10},{9,11},{10,... | collective-permute-start | bytes 589832 | tf_op jit(solution)/shard_map/ppermute | solution.py:353
  7.6 10.9 %collective-permute-start.1 = (bf16[384,256]{1,0:T(8,128)(2,1)S(1)}, bf16[384,256]{1,0:T(8,128)(2,1)S(1)}, u32[]{:S(2)}, u32[]{:S(2)}) collective-permute-start(bf16[384,256]{1,0:T(8,128)(2,1)S(1)} %again.1), channel_id=1, source_target_pairs={{0,16},{16,32},{32,48},{48,64},{64,80},{80,96},{96,112},{112,128},... | collective-permute-start | bytes 589832 | tf_op jit(solution)/shard_map/ppermute | solution.py:353
  9.2 1.1 %copy-start = (bf16[384,1024]{1,0:T(8,128)(2,1)S(1)}, bf16[384,1024]{1,0:T(8,128)(2,1)}, u32[]{:S(2)}) copy-start(bf16[384,1024]{1,0:T(8,128)(2,1)} %refs_0_.1) | copy-start | bytes 2359300
  10.4 1.1 %copy-start.1 = (bf16[384,1024]{1,0:T(8,128)(2,1)S(1)}, bf16[384,1024]{1,0:T(8,128)(2,1)}, u32[]{:S(2)}) copy-start(bf16[384,1024]{1,0:T(8,128)(2,1)} %refs_1_.1) | copy-start | bytes 2359300
  14.3 7.8 %collective-permute-start.3 = (bf16[384,256]{1,0:T(8,128)(2,1)S(1)}, bf16[384,256]{1,0:T(8,128)(2,1)S(1)}, u32[]{:S(2)}, u32[]{:S(2)}) collective-permute-start(bf16[384,256]{1,0:T(8,128)(2,1)S(1)} %collective-permute-done.2.refs_3_.refs_1_), channel_id=1, source_target_pairs={{0,2},{1,3},{2,4},{3,5},{4,6},{5,7},{6,8},{7,9},{8,10},{9,11},{10,... | collective-permute-start | bytes 589832 | tf_op jit(solution)/shard_map/ppermute | solution.py:353
  27.0 7.9 %collective-permute-start.4 = (bf16[384,256]{1,0:T(8,128)(2,1)S(1)}, bf16[384,256]{1,0:T(8,128)(2,1)S(1)}, u32[]{:S(2)}, u32[]{:S(2)}) collective-permute-start(bf16[384,256]{1,0:T(8,128)(2,1)S(1)} %get-tuple-element.48), channel_id=1, source_target_pairs={{0,14},{1,15},{2,0},{3,1},{4,2},{5,3},{6,4},{7,5},{8,6},{9,7},{10,... | collective-permute-start | bytes 589832 | tf_op jit(solution)/shard_map/ppermute | solution.py:353
  30.6 15.5 %collective-permute-start.6 = (bf16[384,256]{1,0:T(8,128)(2,1)S(1)}, bf16[384,256]{1,0:T(8,128)(2,1)S(1)}, u32[]{:S(2)}, u32[]{:S(2)}) collective-permute-start(bf16[384,256]{1,0:T(8,128)(2,1)S(1)} %get-tuple-element.49), channel_id=1, source_target_pairs={{0,14},{1,15},{2,0},{3,1},{4,2},{5,3},{6,4},{7,5},{8,6},{9,7},{10,... | collective-permute-start | bytes 589832 | tf_op jit(solution)/shard_map/ppermute | solution.py:353
  30.6 15.4 %collective-permute-start.7 = (bf16[384,256]{1,0:T(8,128)(2,1)S(1)}, bf16[384,256]{1,0:T(8,128)(2,1)S(1)}, u32[]{:S(2)}, u32[]{:S(2)}) collective-permute-start(bf16[384,256]{1,0:T(8,128)(2,1)S(1)} %get-tuple-element.50), channel_id=1, source_target_pairs={{0,240},{16,0},{32,16},{48,32},{64,48},{80,64},{96,80},{112,96},{1... | collective-permute-start | bytes 589832 | tf_op jit(solution)/shard_map/ppermute | solution.py:353
  35.0 14.2 %collective-permute-start.5 = (bf16[384,256]{1,0:T(8,128)(2,1)S(1)}, bf16[384,256]{1,0:T(8,128)(2,1)S(1)}, u32[]{:S(2)}, u32[]{:S(2)}) collective-permute-start(bf16[384,256]{1,0:T(8,128)(2,1)S(1)} %add_convert_fusion.1), channel_id=1, source_target_pairs={{0,15},{1,0},{2,1},{3,2},{4,3},{5,4},{6,5},{7,6},{8,7},{9,8},{10,9... | collective-permute-start | bytes 589832 | tf_op jit(solution)/shard_map/ppermute | solution.py:353

commit v2 on v1

--- a/solution.py
+++ b/solution.py
@@ -16,7 +16,7 @@
 ROOT = 1.0 / math.sqrt(HEAD)
 SCALE = ROOT * math.log2(math.e)
 BIG = 1e30
-SAFE = 60.0
+SAFE = 100.0
 TILE = 256
 UNROLL = 4
 F32 = jnp.float32
@@ -46,19 +46,26 @@
         gt_ref[pair] = gs_ref[pair].T
         square = turned.astype(F32)
         norm = jnp.maximum(norm, jnp.sum(fold(square * square, jnp.sum), axis=0, keepdims=True))
-    norm_ref[...] = norm
-
-
-def again_kernel(spans_ref, own_ref, out_ref):
+    norm_ref[...] = jnp.broadcast_to(jnp.max(norm, axis=1, keepdims=True), norm_ref.shape)
+
+
+def again_kernel(spans_ref, own_ref, out_ref, bias_ref):
     out_ref[...] = own_ref[...]
+    wide = bias_ref.shape[1]
+    lane = lax.broadcasted_iota(jnp.int32, (1, wide), 1)
+    lane = jnp.where(lane >= wide // 2, lane - wide // 2, lane)
+    qpos = jnp.where(lane < wide // 4, spans_ref[0], spans_ref[1])
+    for n in range(2 * BLOCKS):
+        bias_ref[n : n + 1, :] = jnp.where(qpos >= spans_ref[n], 0.0, BIG)
 
 
 def small(norm_ref, kv_refs):
-    longest = jnp.zeros((kv_refs[0].shape[0], 1), F32)
+    longest = 0.0
     for ref in kv_refs:
         key = ref[:, :HEAD].astype(F32)
-        longest = jnp.maximum(longest, jnp.sum(key * key, axis=1, keepdims=True))
-    return jnp.max(longest) * jnp.max(norm_ref[...]) * (SCALE * SCALE) < SAFE * SAFE
+        longest = jnp.maximum(longest, fold(key * key, jnp.max))
+    longest = jnp.sum(jnp.max(longest, axis=0, keepdims=True))
+    return longest * jnp.max(norm_ref[...]) * (SCALE * SCALE) < SAFE * SAFE
 
 
 def either(safe, make):
@@ -71,21 +78,19 @@
         make(True)
 
 
-def scores(exact, pair, spans_ref, numbers, qt_ref, gt_ref, kv_refs, prob, gprob, mask):
+def scores(exact, pair, bias_ref, numbers, qt_ref, gt_ref, kv_refs, prob, gprob, mask):
     tok = kv_refs[0].shape[0]
     span = tok // 2
     wide = 2 * tok
     found = {}
     for t in range(wide // TILE):
         cols = slice(t * TILE, (t + 1) * TILE)
-        lane = lax.broadcasted_iota(jnp.int32, (1, TILE), 1) + t * TILE
-        qpos = jnp.where((lane % tok) < span, spans_ref[0], spans_ref[1])
         for b, number in enumerate(numbers):
             s = jnp.dot(kv_refs[b][:, :HEAD], qt_ref[pair, :, cols], preferred_element_type=F32)
             g = jnp.dot(kv_refs[b][:, HEAD:], gt_ref[pair, :, cols], preferred_element_type=F32)
             if b == 0 and mask is not None:
                 s = s + mask[:, cols]
-            bias = [jnp.where(qpos >= spans_ref[2 * number + half], 0.0, BIG) for half in range(2)]
+            bias = [bias_ref[2 * number + half : 2 * number + half + 1, cols] for half in range(2)]
             top = jnp.zeros((1, TILE), F32)
             if exact:
                 top = jnp.maximum(fold(s[:span], jnp.max) - bias[0], fold(s[span:], jnp.max) - bias[1])
@@ -129,7 +134,7 @@
     return best, total, product, weights
 
 
-def scores_kernel(numbers, spans_ref, *refs):
+def scores_kernel(numbers, bias_ref, *refs):
     count = len(numbers)
     mask = before = None
     if numbers[0] == 0:
@@ -143,7 +148,7 @@
 
     def make(exact):
         def step(pair, carry):
-            found = scores(exact, pair, spans_ref, numbers, qt_ref, gt_ref, kv_refs, prob, gprob, mask)
+            found = scores(exact, pair, bias_ref, numbers, qt_ref, gt_ref, kv_refs, prob, gprob, mask)
             if before is None:
                 keep(stats, pair, found[0])
             else:
@@ -176,11 +181,11 @@
 
 
 def last_kernel(
-    spans_ref, q_ref, go_ref, qt_ref, gt_ref, norm_ref, stats, kv_ref, rates, dscore, dkv, prob, gprob
+    bias_ref, q_ref, go_ref, qt_ref, gt_ref, norm_ref, stats, kv_ref, rates, dscore, dkv, prob, gprob
 ):
     def make(exact):
         def find(pair, carry):
-            (found,) = scores(exact, pair, spans_ref, [BLOCKS - 1], qt_ref, gt_ref, [kv_ref], prob, gprob, None)
+            (found,) = scores(exact, pair, bias_ref, [BLOCKS - 1], qt_ref, gt_ref, [kv_ref], prob, gprob, None)
             _, total, product, weights = merged([[stats[pair, n : n + 1, :] for n in range(3)], found])
             inv = 1.0 / total
             keep(rates, pair, [weights[0] * inv, product * inv, weights[1] * inv])
@@ -271,19 +276,20 @@
 
 
 def again(spans, kv):
-    return call(again_kernel, "again", [spans, kv], [shape(BF16, *kv.shape)], [], 0)[0]
-
-
-def own_scores(spans, queries, grad_out, kv):
+    out = [shape(BF16, *kv.shape), shape(F32, 16, 2 * kv.shape[0])]
+    return call(again_kernel, "again", [spans, kv], out, [], 0)
+
+
+def own_scores(bias, queries, grad_out, kv):
     tok = kv.shape[0]
     wide = 2 * tok
     return call(
         functools.partial(scores_kernel, [0]),
         "own_scores",
-        [spans, queries, grad_out, kv],
+        [bias, queries, grad_out, kv],
         [shape(BF16, PAIRS, wide, HEAD)] * 2
         + [shape(BF16, PAIRS, HEAD, wide)] * 2
-        + [shape(F32, 8, wide)]
+        + [shape(F32, 8, HEAD)]
         + [shape(BF16, PAIRS, tok, wide)] * 2
         + [shape(F32, PAIRS, 8, wide)],
         [pltpu.VMEM((tok, wide), F32)],
@@ -291,26 +297,26 @@
     )
 
 
-def score(name, spans, qt, gt, norm, blocks, numbers, *before):
+def score(name, bias, qt, gt, norm, blocks, numbers, *before):
     tok = blocks[0].shape[0]
     keys, wide = len(blocks) * tok, 2 * tok
     return call(
         functools.partial(scores_kernel, numbers),
         name,
-        [spans, qt, gt, norm, *blocks, *before],
+        [bias, qt, gt, norm, *blocks, *before],
         [shape(BF16, PAIRS, keys, wide), shape(BF16, PAIRS, keys, wide), shape(F32, PAIRS, 8, wide)],
         [],
         work(tok, len(blocks), 2),
     )
 
 
-def last(spans, queries, grad_out, qt, gt, norm, stats, kv):
+def last(bias, queries, grad_out, qt, gt, norm, stats, kv):
     tok = queries.shape[1] // 2
     wide = 2 * tok
     return call(
         last_kernel,
         "last_block",
-        [spans, queries, grad_out, qt, gt, norm, stats, kv],
+        [bias, queries, grad_out, qt, gt, norm, stats, kv],
         [shape(F32, PAIRS, 8, wide), shape(BF16, PAIRS, tok, wide), shape(BF16, tok, 2 * HEAD)],
         [pltpu.VMEM((PAIRS, tok, wide), BF16)] * 2,
         work(tok, 1, 4),
@@ -367,15 +373,15 @@
     numbers = [outer_index * inner_count + (inner_index - stride) % inner_count for stride in range(STEPS)]
     numbers.insert(3, (outer_index - 1) % outer_count * inner_count + inner_index)
     spans = jnp.concatenate([lax.dynamic_slice_in_dim(span_order, 2 * n, 2, 0) for n in numbers])
-    later = again(spans, own)
+    later, bias = again(spans, own)
     second = rotate(later, "inner", 2)
     outer = rotate(later, "outer", 1)
     third = rotate(first, "inner", 2)
 
-    queries, grad_out, *turns, e0, g0, s0 = own_scores(spans, queries, grad_out, own)
-    e1, g1, near = score("first_scores", spans, *turns, [first], [1], s0)
-    e2, g2, far = score("two_scores", spans, *turns, [second, outer], [2, 3], near)
-    rates, ds3, p_third = last(spans, queries, grad_out, *turns, far, third)
+    queries, grad_out, *turns, e0, g0, s0 = own_scores(bias, queries, grad_out, own)
+    e1, g1, near = score("first_scores", bias, *turns, [first], [1], s0)
+    e2, g2, far = score("two_scores", bias, *turns, [second, outer], [2, 3], near)
+    rates, ds3, p_third = last(bias, queries, grad_out, *turns, far, third)
     third_back = rotate(p_third, "inner", -2)
     stats = (rates, near, far)
     ds2, p_second, p_outer = block_grads("two_grads", queries, grad_out, *stats, e2, g2, [[(1, 4)], [(1, 5)]])

time: 50.2 us -> 48.3 us (0.962)
  Pallas kernels: 23.6 us -> 18.8 us
  starting transfers between devices: 14.8 us -> 17 us
  waiting for transfers between devices: 5.76 us -> 6.42 us
    pallas_call x8, Pallas kernels: 23.6 us -> 18.8 us  [call(): pl.pallas_call(kernel, name=name, out_shape=outs, in_specs=[SMEM if x.dty...]
    ppermute x8, starting transfers between devices: 14.8 us -> 17 us  [rotate(): lax.ppermute(value, axis, [(i, (i + by) % size) for i in range(size)])]
    ppermute x8, waiting for transfers between devices: 5.76 us -> 6.42 us  [rotate(): lax.ppermute(value, axis, [(i, (i + by) % size) for i in range(size)])]
  transfers between devices with their start and end apart: 8 -> 8, of which waited for: 2 -> 3; matrix products, arithmetic and copies ran while one was open for 2% -> 2% of each run, Pallas kernels for 38% -> 33%
where the time goes in v2:
time: 48.3 us; the launch traced here: 48.1 us
  Pallas kernels  18.8 us (39%)
  starting transfers between devices  17 us (35%)
  waiting for transfers between devices  6.42 us (13%)
  local copies, waits for them, and re-layouts  3.98 us (8%)
  other arithmetic  1.12 us (2%)
  between operations  0.73 us (2%)
    pallas_call x8, Pallas kernels, call(): pl.pallas_call(kernel, name=name, out_shape=outs, in_specs=[SMEM if x.dty...  18.8 us
    ppermute x8, starting transfers between devices, rotate(): lax.ppermute(value, axis, [(i, (i + by) % size) for i in range(size)])  17 us
    ppermute x8, waiting for transfers between devices, rotate(): lax.ppermute(value, axis, [(i, (i + by) % size) for i in range(size)])  6.42 us
    unnamed x4, local copies, waits for them, and re-layouts  2.27 us
    select_n x1, other arithmetic, body(): jnp.where(left, lax.pad(keys, zero, ((0, 0, 0), (0, HEAD, 0))), lax.pad(v...  0.98 us
  transfers between devices with their start and end apart: 8, of which 3 were waited for; matrix products, arithmetic and copies ran while one was open for 2% of the time, Pallas kernels for 33%

profile of v2, /device:TPU:123, one launch (start us, length us, event | category | flops | bytes accessed | tf_op | source)
XLA Modules:
  0.0 48.1 jit_solution(12845217252538172133)
XLA Ops:
  0.6 1.0 %pad_select_fusion.own_ref.refs_2_.refs_0_ = bf16[384,256]{1,0:T(8,128)(2,1)S(1)} fusion(bf16[384,128]{1,0:T(8,128)(2,1)} %param.7, bf16[384,128]{1,0:T(8,128)(2,1)} %param.6, pred[256]{0:T(512)(128)(4,1)S(1)} %iota_compare_fusion), kind=kLoop, calls=%fused_computation.2 | loop fusion | flops 98304 | bytes 393472 | tf_op jit(solution)/shard_map/jit(_where)/select_n | solution.py:369
  1.6 3.6 %collective-permute-start.2 = (bf16[384,256]{1,0:T(8,128)(2,1)S(1)}, bf16[384,256]{1,0:T(8,128)(2,1)S(1)}, u32[]{:S(2)}, u32[]{:S(2)}) collective-permute-start(bf16[384,256]{1,0:T(8,128)(2,1)S(1)} %pad_select_fusion.own_ref.refs_2_.refs_0_), channel_id=1, source_target_pairs={{0,1},{1,2},{2,3},{3,4},{4,5},{5,6},{6,7},{7,8},{8,9},{9,10},{10,1... | collective-permute-start | bytes 589832 | tf_op jit(solution)/shard_map/ppermute | solution.py:359
  5.2 0.9 %fusion.1 = (s32[2]{0:T(128)S(1)}, s32[2]{0:T(128)S(1)}, s32[2]{0:T(128)S(1)}, s32[2]{0:T(128)S(1)}, s32[2]{0:T(128)S(1)}) fusion(s32[512]{0:T(512)} %param.9, s32[]{:T(128)S(6)} %select_n.51, s32[]{:T(128)S(6)} %select_n.47, s32[]{:T(128)S(6)} %select_n.45, s32[]{:T(128)S(6)} %select_n.43, s32[]{:T(128)S(6)} %select_n.49), kind=kLoop, calls=%fused_computation.5 | loop fusion | bytes 100 | tf_op jit(solution)/shard_map/dynamic_slice | solution.py:375
  6.2 0.1 concatenate.3.spans_ref
  6.2 0.6 %again.1 = (bf16[384,256]{1,0:T(8,128)(2,1)S(1)}, f32[16,768]{1,0:T(8,128)S(1)}) custom-call(s32[10]{0:T(128)S(1)} %concatenate.3.spans_ref, bf16[384,256]{1,0:T(8,128)(2,1)S(1)} %pad_select_fusion.own_ref.refs_2_.refs_0_), custom_call_target="tpu_custom_call" | custom-call | tf_op jit(solution)/shard_map/again/pallas_call | solution.py:262
  6.8 0.8 %collective-permute-start = (bf16[384,256]{1,0:T(8,128)(2,1)S(1)}, bf16[384,256]{1,0:T(8,128)(2,1)S(1)}, u32[]{:S(2)}, u32[]{:S(2)}) collective-permute-start(bf16[384,256]{1,0:T(8,128)(2,1)S(1)} %get-tuple-element.35), channel_id=1, source_target_pairs={{0,2},{1,3},{2,4},{3,5},{4,6},{5,7},{6,8},{7,9},{8,10},{9,11},{10,... | collective-permute-start | bytes 589832 | tf_op jit(solution)/shard_map/ppermute | solution.py:359
  7.6 1.6 %collective-permute-start.1 = (bf16[384,256]{1,0:T(8,128)(2,1)S(1)}, bf16[384,256]{1,0:T(8,128)(2,1)S(1)}, u32[]{:S(2)}, u32[]{:S(2)}) collective-permute-start(bf16[384,256]{1,0:T(8,128)(2,1)S(1)} %get-tuple-element.35), channel_id=1, source_target_pairs={{0,16},{16,32},{32,48},{48,64},{64,80},{80,96},{96,112},{112,128},... | collective-permute-start | bytes 589832 | tf_op jit(solution)/shard_map/ppermute | solution.py:359
  9.3 0.0 copy-start
  9.3 1.1 %copy-done = bf16[384,1024]{1,0:T(8,128)(2,1)S(1)} copy-done((bf16[384,1024]{1,0:T(8,128)(2,1)S(1)}, bf16[384,1024]{1,0:T(8,128)(2,1)}, u32[]{:S(2)}) %copy-start) | copy-done | bytes 786456
  10.4 0.0 copy-start.1
  10.4 1.1 %copy-done.1 = bf16[384,1024]{1,0:T(8,128)(2,1)S(1)} copy-done((bf16[384,1024]{1,0:T(8,128)(2,1)S(1)}, bf16[384,1024]{1,0:T(8,128)(2,1)}, u32[]{:S(2)}) %copy-start.1) | copy-done | bytes 786456
  11.5 2.3 %own_scores.1 = (bf16[4,768,128]{2,1,0:T(8,128)(2,1)S(1)}, bf16[4,768,128]{2,1,0:T(8,128)(2,1)S(1)}, bf16[4,128,768]{2,1,0:T(8,128)(2,1)S(1)}, bf16[4,128,768]{2...) custom-call(f32[16,768]{1,0:T(8,128)S(1)} %get-tuple-element.29.bias, ...), custom_call_target="tpu_custom_call" | custom-call | flops 1207959552 | tf_op jit(solution)/shard_map/own_scores/pallas_call | solution.py:262
  13.8 0.0 collective-permute-done.2.refs_3_.refs_1_
  13.9 0.8 %collective-permute-start.3 = (bf16[384,256]{1,0:T(8,128)(2,1)S(1)}, bf16[384,256]{1,0:T(8,128)(2,1)S(1)}, u32[]{:S(2)}, u32[]{:S(2)}) collective-permute-start(bf16[384,256]{1,0:T(8,128)(2,1)S(1)} %collective-permute-done.2.refs_3_.refs_1_), channel_id=1, source_target_pairs={{0,2},{1,3},{2,4},{3,5},{4,6},{5,7},{6,8},{7,9},{8,10},{9,11},{10,... | collective-permute-start | bytes 589832 | tf_op jit(solution)/shard_map/ppermute | solution.py:359
  14.7 1.6 %first_scores.1 = (bf16[4,384,768]{2,1,0:T(8,128)(2,1)S(1)}, bf16[4,384,768]{2,1,0:T(8,128)(2,1)S(1)}, f32[4,8,768]{2,1,0:T(8,128)S(1)}) custom-call(f32[16,768]{1,0:T(8,128)S(1)} %get-tuple-element.29.bias_ref, bf16[4,128,768]{2,1,0:T(8,128)(2,1)S(1)} %get-tuple-element.32.refs_0_.qt_ref, bf16[4,128,768]{2,1,0:T(8,128)(2,1)S(1)} %get-tuple-element.33.refs_1_.gt_ref, ...), custom_call_target="tpu_custom_call" | custom-call | flops 1207959552 | tf_op jit(solution)/shard_map/first_scores/pallas_call | solution.py:262
  16.2 0.0 collective-permute-done.refs_3_.refs_2_
  16.2 0.0 collective-permute-done.1.refs_4_.refs_3_
  16.3 3.0 %two_scores.1 = (bf16[4,768,768]{2,1,0:T(8,128)(2,1)S(1)}, bf16[4,768,768]{2,1,0:T(8,128)(2,1)S(1)}, f32[4,8,768]{2,1,0:T(8,128)S(1)}) custom-call(f32[16,768]{1,0:T(8,128)S(1)} %get-tuple-element.29.bias_ref, bf16[4,128,768]{2,1,0:T(8,128)(2,1)S(1)} %get-tuple-element.32.refs_0_.qt_ref, bf16[4,128,768]{2,1,0:T(8,128)(2,1)S(1)} %get-tuple-element.33.refs_1_.gt_ref, ...), custom_call_target="tpu_custom_call" | custom-call | flops 2415919104 | tf_op jit(solution)/shard_map/two_scores/pallas_call | solution.py:262
  19.3 1.5 %collective-permute-done.3.kv_ref.refs_4_ = bf16[384,256]{1,0:T(8,128)(2,1)S(1)} collective-permute-done((bf16[384,256]{1,0:T(8,128)(2,1)S(1)}, bf16[384,256]{1,0:T(8,128)(2,1)S(1)}, u32[]{:S(2)}, u32[]{:S(2)}) %collective-permute-start.3) | collective-permute-done | bytes 196640 | tf_op jit(solution)/shard_map/ppermute | solution.py:359
  20.8 3.0 %last_block.1 = (f32[4,8,768]{2,1,0:T(8,128)S(1)}, bf16[4,384,768]{2,1,0:T(8,128)(2,1)S(1)}, bf16[384,256]{1,0:T(8,128)(2,1)S(1)}) custom-call(f32[16,768]{1,0:T(8,128)S(1)} %get-tuple-element.29.bias_ref, bf16[4,768,128]{2,1,0:T(8,128)(2,1)S(1)} %get-tuple-element.30.q_ref, bf16[4,768,128]{2,1,0:T(8,128)(2,1)S(1)} %get-tuple-element.31.go_ref, ...), custom_call_target="tpu_custom_call" | custom-call | flops 2415919104 | tf_op jit(solution)/shard_map/last_block/pallas_call | solution.py:262
  23.8 0.8 %collective-permute-start.4 = (bf16[384,256]{1,0:T(8,128)(2,1)S(1)}, bf16[384,256]{1,0:T(8,128)(2,1)S(1)}, u32[]{:S(2)}, u32[]{:S(2)}) collective-permute-start(bf16[384,256]{1,0:T(8,128)(2,1)S(1)} %get-tuple-element.52), channel_id=1, source_target_pairs={{0,14},{1,15},{2,0},{3,1},{4,2},{5,3},{6,4},{7,5},{8,6},{9,7},{10,... | collective-permute-start | bytes 589832 | tf_op jit(solution)/shard_map/ppermute | solution.py:359
  24.6 2.8 %two_grads.1 = (bf16[4,768,768]{2,1,0:T(8,128)(2,1)S(1)}, bf16[384,256]{1,0:T(8,128)(2,1)S(1)}, bf16[384,256]{1,0:T(8,128)(2,1)S(1)}) custom-call(bf16[4,768,128]{2,1,0:T(8,128)(2,1)S(1)} %get-tuple-element.30.q_ref, bf16[4,768,128]{2,1,0:T(8,128)(2,1)S(1)} %get-tuple-element.31.go_ref, f32[4,8,768]{2,1,0:T(8,128)S(1)} %get-tuple-element.39.rates, ...), custom_call_target="tpu_custom_call" | custom-call | flops 2415919104 | tf_op jit(solution)/shard_map/two_grads/pallas_call | solution.py:262
  27.4 0.1 collective-permute-start.6
  27.4 0.8 %collective-permute-start.7 = (bf16[384,256]{1,0:T(8,128)(2,1)S(1)}, bf16[384,256]{1,0:T(8,128)(2,1)S(1)}, u32[]{:S(2)}, u32[]{:S(2)}) collective-permute-start(bf16[384,256]{1,0:T(8,128)(2,1)S(1)} %get-tuple-element.54), channel_id=1, source_target_pairs={{0,240},{16,0},{32,16},{48,32},{64,48},{80,64},{96,80},{112,96},{1... | collective-permute-start | bytes 589832 | tf_op jit(solution)/shard_map/ppermute | solution.py:359
  28.3 1.4 %first_grads.1 = (bf16[4,384,768]{2,1,0:T(8,128)(2,1)S(1)}, bf16[384,256]{1,0:T(8,128)(2,1)S(1)}) custom-call(bf16[4,768,128]{2,1,0:T(8,128)(2,1)S(1)} %get-tuple-element.30.q_ref, bf16[4,768,128]{2,1,0:T(8,128)(2,1)S(1)} %get-tuple-element.31.go_ref, f32[4,8,768]{2,1,0:T(8,128)S(1)} %get-tuple-element.39.rates, ...), custom_call_target="tpu_custom_call" | custom-call | flops 1207959552 | tf_op jit(solution)/shard_map/first_grads/pallas_call | solution.py:262
  29.7 1.3 %collective-permute-done.4 = bf16[384,256]{1,0:T(8,128)(2,1)S(1)} collective-permute-done((bf16[384,256]{1,0:T(8,128)(2,1)S(1)}, bf16[384,256]{1,0:T(8,128)(2,1)S(1)}, u32[]{:S(2)}, u32[]{:S(2)}) %collective-permute-start.4) | collective-permute-done | bytes 196640 | tf_op jit(solution)/shard_map/ppermute | solution.py:359
  31.1 8.4 %collective-permute-start.5 = (bf16[384,256]{1,0:T(8,128)(2,1)S(1)}, bf16[384,256]{1,0:T(8,128)(2,1)S(1)}, u32[]{:S(2)}, u32[]{:S(2)}) collective-permute-start(bf16[384,256]{1,0:T(8,128)(2,1)S(1)} %add_convert_fusion.1), channel_id=1, source_target_pairs={{0,15},{1,0},{2,1},{3,2},{4,3},{5,4},{6,5},{7,6},{8,7},{9,8},{10,9... | collective-permute-start | bytes 589832 | tf_op jit(solution)/shard_map/ppermute | solution.py:359
  39.5 4.2 %own_grads.1 = (bf16[384,1024]{1,0:T(8,128)(2,1)}, f32[384,256]{1,0:T(8,128)S(1)}) custom-call(bf16[4,768,128]{2,1,0:T(8,128)(2,1)S(1)} %get-tuple-element.30.q_ref, bf16[4,768,128]{2,1,0:T(8,128)(2,1)S(1)} %get-tuple-element.31.go_ref, f32[4,8,768]{2,1,0:T(8,128)S(1)} %get-tuple-element.39.rates, f32[4,8,768]{2,1,0:T(8,128)S(1)} %get-tuple-element.37.refs_5_.refs_0_.near, ...), custom_call_target="tpu_custom_call" | custom-call | flops 6039797760 | tf_op jit(solution)/shard_map/own_grads/pallas_call | solution.py:262
  43.7 0.0 collective-permute-done.6
  43.7 0.0 collective-permute-done.7
  43.7 3.6 %collective-permute-done.5 = bf16[384,256]{1,0:T(8,128)(2,1)S(1)} collective-permute-done((bf16[384,256]{1,0:T(8,128)(2,1)S(1)}, bf16[384,256]{1,0:T(8,128)(2,1)S(1)}, u32[]{:S(2)}, u32[]{:S(2)}) %collective-permute-start.5) | collective-permute-done | bytes 196640 | tf_op jit(solution)/shard_map/ppermute | solution.py:359
  47.3 0.1 add_convert_fusion
  47.4 0.7 %fusion = (bf16[384,128]{1,0:T(8,128)(2,1)}, bf16[384,128]{1,0:T(8,128)(2,1)}) fusion(bf16[384,256]{1,0:T(8,128)(2,1)S(1)} %add_convert_fusion), kind=kLoop, calls=%fused_computation.4 | loop fusion | bytes 393216 | tf_op jit(solution)/shard_map/slice | solution.py:396
  (2 shorter events, 0.1 us)
Async XLA Ops:
  1.6 12.2 %collective-permute-start.2 = (bf16[384,256]{1,0:T(8,128)(2,1)S(1)}, bf16[384,256]{1,0:T(8,128)(2,1)S(1)}, u32[]{:S(2)}, u32[]{:S(2)}) collective-permute-start(bf16[384,256]{1,0:T(8,128)(2,1)S(1)} %pad_select_fusion.own_ref.refs_2_.refs_0_), channel_id=1, source_target_pairs={{0,1},{1,2},{2,3},{3,4},{4,5},{5,6},{6,7},{7,8},{8,9},{9,10},{10,1... | collective-permute-start | bytes 589832 | tf_op jit(solution)/shard_map/ppermute | solution.py:359
  6.8 9.4 %collective-permute-start = (bf16[384,256]{1,0:T(8,128)(2,1)S(1)}, bf16[384,256]{1,0:T(8,128)(2,1)S(1)}, u32[]{:S(2)}, u32[]{:S(2)}) collective-permute-start(bf16[384,256]{1,0:T(8,128)(2,1)S(1)} %get-tuple-element.35), channel_id=1, source_target_pairs={{0,2},{1,3},{2,4},{3,5},{4,6},{5,7},{6,8},{7,9},{8,10},{9,11},{10,... | collective-permute-start | bytes 589832 | tf_op jit(solution)/shard_map/ppermute | solution.py:359
  7.6 8.6 %collective-permute-start.1 = (bf16[384,256]{1,0:T(8,128)(2,1)S(1)}, bf16[384,256]{1,0:T(8,128)(2,1)S(1)}, u32[]{:S(2)}, u32[]{:S(2)}) collective-permute-start(bf16[384,256]{1,0:T(8,128)(2,1)S(1)} %get-tuple-element.35), channel_id=1, source_target_pairs={{0,16},{16,32},{32,48},{48,64},{64,80},{80,96},{96,112},{112,128},... | collective-permute-start | bytes 589832 | tf_op jit(solution)/shard_map/ppermute | solution.py:359
  9.3 1.1 %copy-start = (bf16[384,1024]{1,0:T(8,128)(2,1)S(1)}, bf16[384,1024]{1,0:T(8,128)(2,1)}, u32[]{:S(2)}) copy-start(bf16[384,1024]{1,0:T(8,128)(2,1)} %refs_0_.1) | copy-start | bytes 2359300
  10.4 1.1 %copy-start.1 = (bf16[384,1024]{1,0:T(8,128)(2,1)S(1)}, bf16[384,1024]{1,0:T(8,128)(2,1)}, u32[]{:S(2)}) copy-start(bf16[384,1024]{1,0:T(8,128)(2,1)} %refs_1_.1) | copy-start | bytes 2359300
  13.9 6.9 %collective-permute-start.3 = (bf16[384,256]{1,0:T(8,128)(2,1)S(1)}, bf16[384,256]{1,0:T(8,128)(2,1)S(1)}, u32[]{:S(2)}, u32[]{:S(2)}) collective-permute-start(bf16[384,256]{1,0:T(8,128)(2,1)S(1)} %collective-permute-done.2.refs_3_.refs_1_), channel_id=1, source_target_pairs={{0,2},{1,3},{2,4},{3,5},{4,6},{5,7},{6,8},{7,9},{8,10},{9,11},{10,... | collective-permute-start | bytes 589832 | tf_op jit(solution)/shard_map/ppermute | solution.py:359
  23.8 7.3 %collective-permute-start.4 = (bf16[384,256]{1,0:T(8,128)(2,1)S(1)}, bf16[384,256]{1,0:T(8,128)(2,1)S(1)}, u32[]{:S(2)}, u32[]{:S(2)}) collective-permute-start(bf16[384,256]{1,0:T(8,128)(2,1)S(1)} %get-tuple-element.52), channel_id=1, source_target_pairs={{0,14},{1,15},{2,0},{3,1},{4,2},{5,3},{6,4},{7,5},{8,6},{9,7},{10,... | collective-permute-start | bytes 589832 | tf_op jit(solution)/shard_map/ppermute | solution.py:359
  27.4 16.4 %collective-permute-start.6 = (bf16[384,256]{1,0:T(8,128)(2,1)S(1)}, bf16[384,256]{1,0:T(8,128)(2,1)S(1)}, u32[]{:S(2)}, u32[]{:S(2)}) collective-permute-start(bf16[384,256]{1,0:T(8,128)(2,1)S(1)} %get-tuple-element.53), channel_id=1, source_target_pairs={{0,14},{1,15},{2,0},{3,1},{4,2},{5,3},{6,4},{7,5},{8,6},{9,7},{10,... | collective-permute-start | bytes 589832 | tf_op jit(solution)/shard_map/ppermute | solution.py:359
  27.4 16.3 %collective-permute-start.7 = (bf16[384,256]{1,0:T(8,128)(2,1)S(1)}, bf16[384,256]{1,0:T(8,128)(2,1)S(1)}, u32[]{:S(2)}, u32[]{:S(2)}) collective-permute-start(bf16[384,256]{1,0:T(8,128)(2,1)S(1)} %get-tuple-element.54), channel_id=1, source_target_pairs={{0,240},{16,0},{32,16},{48,32},{64,48},{80,64},{96,80},{112,96},{1... | collective-permute-start | bytes 589832 | tf_op jit(solution)/shard_map/ppermute | solution.py:359
  31.1 16.2 %collective-permute-start.5 = (bf16[384,256]{1,0:T(8,128)(2,1)S(1)}, bf16[384,256]{1,0:T(8,128)(2,1)S(1)}, u32[]{:S(2)}, u32[]{:S(2)}) collective-permute-start(bf16[384,256]{1,0:T(8,128)(2,1)S(1)} %add_convert_fusion.1), channel_id=1, source_target_pairs={{0,15},{1,0},{2,1},{3,2},{4,3},{5,4},{6,5},{7,6},{8,7},{9,8},{10,9... | collective-permute-start | bytes 589832 | tf_op jit(solution)/shard_map/ppermute | solution.py:359

commit v3 on v2

--- a/solution.py
+++ b/solution.py
@@ -36,11 +36,11 @@
     return jnp.concatenate([ref[:, pl.ds(first, HEAD)], ref[:, pl.ds(second, HEAD)]], axis=0)
 
 
-def turn(q_ref, go_ref, qs_ref, gs_ref, qt_ref, gt_ref, norm_ref):
-    norm = jnp.zeros((8, 2 * q_ref.shape[0]), F32)
+def turn(both_ref, qs_ref, gs_ref, qt_ref, gt_ref, norm_ref):
+    norm = jnp.zeros((8, 2 * both_ref.shape[0]), F32)
     for pair in range(PAIRS):
-        qs_ref[pair] = heads_of(q_ref, pair)
-        gs_ref[pair] = heads_of(go_ref, pair)
+        qs_ref[pair] = heads_of(both_ref, pair)
+        gs_ref[pair] = heads_of(both_ref, PAIRS + pair)
         turned = qs_ref[pair].T
         qt_ref[pair] = turned
         gt_ref[pair] = gs_ref[pair].T
@@ -138,9 +138,9 @@
     count = len(numbers)
     mask = before = None
     if numbers[0] == 0:
-        q_ref, go_ref, kv_ref, qs_ref, gs_ref, qt_ref, gt_ref, norm_ref, prob, gprob, stats, mask = refs
+        both_ref, kv_ref, qs_ref, gs_ref, qt_ref, gt_ref, norm_ref, prob, gprob, stats, mask = refs
         kv_refs = [kv_ref]
-        turn(q_ref, go_ref, qs_ref, gs_ref, qt_ref, gt_ref, norm_ref)
+        turn(both_ref, qs_ref, gs_ref, qt_ref, gt_ref, norm_ref)
         diagonal(mask)
     else:
         qt_ref, gt_ref, norm_ref = refs[:3]
@@ -161,13 +161,14 @@
     either(small(norm_ref, kv_refs), make)
 
 
-def grads(pair, q_ref, go_ref, rates, rowdot, prob, gprob, dscore, dk, dv):
+def grads(pair, q_ref, go_ref, rates, rowdot, prob, gprob, dscore, dk, dv, base=0):
     tok = q_ref.shape[1] // 2
     q, go = q_ref[pair], go_ref[pair]
     for b, rate in enumerate(rates):
         rows = slice(b * tok, (b + 1) * tok)
-        p = prob[pair, rows, :].astype(F32) * rate
-        ds = (p * (gprob[pair, rows, :].astype(F32) - rowdot)).astype(BF16)
+        given = slice((base + b) * tok, (base + b + 1) * tok)
+        p = prob[pair, given, :].astype(F32) * rate
+        ds = (p * (gprob[pair, given, :].astype(F32) - rowdot)).astype(BF16)
         dscore[pair, rows, :] = ds
         dk[rows, :] += jnp.dot(ds, q, preferred_element_type=F32)
         dv[rows, :] += jnp.dot(p.astype(BF16), go, preferred_element_type=F32)
@@ -208,7 +209,7 @@
     dkv[:, HEAD:] = dv.astype(BF16)
 
 
-def grads_kernel(chains, q_ref, go_ref, rates, *refs):
+def grads_kernel(chains, base, q_ref, go_ref, rates, *refs):
     stats, (prob, gprob, dscore), outs, (dk, dv) = refs[:2], refs[2:5], refs[5:-2], refs[-2:]
     dk[...] = jnp.zeros_like(dk)
     dv[...] = jnp.zeros_like(dv)
@@ -220,15 +221,16 @@
             for which, row in chain:
                 rate = rate * stats[which][pair, row : row + 1, :]
             each.append(rate)
-        grads(pair, q_ref, go_ref, each, rates[pair, 1:2, :], prob, gprob, dscore, dk, dv)
+        grads(pair, q_ref, go_ref, each, rates[pair, 1:2, :], prob, gprob, dscore, dk, dv, base)
         return carry
 
     lax.fori_loop(0, PAIRS, step, 0, unroll=UNROLL)
     finish(dk, dv, outs)
 
 
-def own_kernel(q_ref, go_ref, rates, near, far, prob, gprob, ds_first, ds_two, ds_last, *refs):
-    kv_refs, (dq_ref, dkv, kt, dscore, dk, dv) = refs[:BLOCKS], refs[BLOCKS:]
+def own_kernel(q_ref, go_ref, rates, near, far, prob, gprob, *refs):
+    kv_refs, (dq_ref, dkv, kt, dscore, dk, dv) = refs[-6 - BLOCKS : -6], refs[-6:]
+    others = refs[: -6 - BLOCKS]
     tok = dkv.shape[0]
     dk[...] = jnp.zeros_like(dk)
     dv[...] = jnp.zeros_like(dv)
@@ -239,7 +241,7 @@
         rate = near[pair, 3:4, :] * far[pair, 3:4, :] * rates[pair, 0:1, :]
         grads(pair, q_ref, go_ref, [rate], rates[pair, 1:2, :], prob, gprob, dscore, dk, dv)
         dqt, start = 0.0, 0
-        for part in (dscore, ds_first, ds_two, ds_last):
+        for part in (dscore, *others):
             end = start + part.shape[1]
             dqt = dqt + jnp.dot(kt[:, start:end], part[pair], preferred_element_type=F32)
             start = end
@@ -280,13 +282,13 @@
     return call(again_kernel, "again", [spans, kv], out, [], 0)
 
 
-def own_scores(bias, queries, grad_out, kv):
+def own_scores(bias, both, kv):
     tok = kv.shape[0]
     wide = 2 * tok
     return call(
         functools.partial(scores_kernel, [0]),
         "own_scores",
-        [bias, queries, grad_out, kv],
+        [bias, both, kv],
         [shape(BF16, PAIRS, wide, HEAD)] * 2
         + [shape(BF16, PAIRS, HEAD, wide)] * 2
         + [shape(F32, 8, HEAD)]
@@ -323,16 +325,16 @@
     )
 
 
-def block_grads(name, queries, grad_out, rates, near, far, prob, gprob, chains):
+def block_grads(name, queries, grad_out, rates, near, far, prob, gprob, chains, base=0):
     tok = queries.shape[1] // 2
-    keys, wide = prob.shape[1:]
-    count = keys // tok
+    wide = prob.shape[2]
+    count = len(chains)
     return call(
-        functools.partial(grads_kernel, chains),
+        functools.partial(grads_kernel, chains, base),
         name,
         [queries, grad_out, rates, near, far, prob, gprob],
-        [shape(BF16, PAIRS, keys, wide)] + [shape(BF16, tok, 2 * HEAD)] * count,
-        [pltpu.VMEM((keys, HEAD), F32)] * 2,
+        [shape(BF16, PAIRS, count * tok, wide)] + [shape(BF16, tok, 2 * HEAD)] * count,
+        [pltpu.VMEM((count * tok, HEAD), F32)] * 2,
         work(tok, count, 2),
     )
 
@@ -359,16 +361,21 @@
     return lax.ppermute(value, axis, [(i, (i + by) % size) for i in range(size)])
 
 
+def side_by_side(one, other):
+    lanes = one.shape[1]
+    zero = jnp.zeros((), one.dtype)
+    left = lax.broadcasted_iota(jnp.int32, (one.shape[0], 2 * lanes), 1) < lanes
+    return jnp.where(
+        left, lax.pad(one, zero, ((0, 0, 0), (0, lanes, 0))), lax.pad(other, zero, ((0, 0, 0), (lanes, 0, 0)))
+    )
+
+
 def body(queries, keys, values, grad_out, span_order):
     inner_count = lax.axis_size("inner")
     outer_count = lax.axis_size("outer")
     outer_index = lax.axis_index("outer")
     inner_index = lax.axis_index("inner")
-    left = lax.broadcasted_iota(jnp.int32, (keys.shape[0], 2 * HEAD), 1) < HEAD
-    zero = jnp.zeros((), BF16)
-    own = jnp.where(
-        left, lax.pad(keys, zero, ((0, 0, 0), (0, HEAD, 0))), lax.pad(values, zero, ((0, 0, 0), (HEAD, 0, 0)))
-    )
+    own = side_by_side(keys, values)
     first = rotate(own, "inner", 1)
     numbers = [outer_index * inner_count + (inner_index - stride) % inner_count for stride in range(STEPS)]
     numbers.insert(3, (outer_index - 1) % outer_count * inner_count + inner_index)
@@ -378,20 +385,23 @@
     outer = rotate(later, "outer", 1)
     third = rotate(first, "inner", 2)
 
-    queries, grad_out, *turns, e0, g0, s0 = own_scores(bias, queries, grad_out, own)
+    queries, grad_out, *turns, e0, g0, s0 = own_scores(bias, side_by_side(queries, grad_out), own)
     e1, g1, near = score("first_scores", bias, *turns, [first], [1], s0)
     e2, g2, far = score("two_scores", bias, *turns, [second, outer], [2, 3], near)
     rates, ds3, p_third = last(bias, queries, grad_out, *turns, far, third)
     third_back = rotate(p_third, "inner", -2)
     stats = (rates, near, far)
-    ds2, p_second, p_outer = block_grads("two_grads", queries, grad_out, *stats, e2, g2, [[(1, 4)], [(1, 5)]])
+    ds2, p_outer = block_grads("outer_grads", queries, grad_out, *stats, e2, g2, [[(1, 5)]], 1)
+    outer_back = rotate(p_outer, "outer", -1)
+    e4, ds2 = lax.optimization_barrier((e2, ds2))
+    ds4, p_second = block_grads("second_grads", queries, grad_out, *stats, e4, g2, [[(1, 4)]], 0)
     second_back = rotate(p_second, "inner", -2)
-    outer_back = rotate(p_outer, "outer", -1)
+    e1, ds4 = lax.optimization_barrier((e1, ds4))
     ds1, p_first = block_grads("first_grads", queries, grad_out, *stats, e1, g1, [[(0, 4), (1, 3)]])
     chain = (p_first.astype(F32) + third_back.astype(F32)).astype(BF16)
     chain_back = rotate(chain, "inner", -1)
-    blocks = [own, first, second, outer, third]
-    grad_q, p_own = own_grads(queries, grad_out, *stats, e0, g0, [ds1, ds2, ds3], blocks)
+    blocks = [own, first, outer, second, third]
+    grad_q, p_own = own_grads(queries, grad_out, *stats, e0, g0, [ds1, ds2, ds4, ds3], blocks)
     summed = p_own + chain_back.astype(F32) + second_back.astype(F32) + outer_back.astype(F32)
     return (grad_q, summed[:, :HEAD].astype(BF16), summed[:, HEAD:].astype(BF16))
 

time: 48.3 us -> 47.3 us (0.979)
  local copies, waits for them, and re-layouts: 3.98 us -> 1.71 us
  other arithmetic: 1.12 us -> 2.88 us
  waiting for transfers between devices: 6.42 us -> 5.77 us
    unnamed x4 -> x0, local copies, waits for them, and re-layouts: 2.27 us -> none
    select_n x1 -> x2, other arithmetic: 0.98 us -> 2.74 us  [side_by_side(): jnp.where(left, lax.pad(one, zero, ((0, 0, 0), (0, lanes, 0))), lax.pad(o...]
    ppermute x8, waiting for transfers between devices: 6.42 us -> 5.77 us  [rotate(): lax.ppermute(value, axis, [(i, (i + by) % size) for i in range(size)])]
    pallas_call x8 -> x9, Pallas kernels: 18.8 us -> 19.1 us  [call(): pl.pallas_call(kernel, name=name, out_shape=outs, in_specs=[SMEM if x.dty...]
  transfers between devices with their start and end apart: 8 -> 8, of which waited for: 3 -> 3; matrix products, arithmetic and copies ran while one was open for 2% -> 6% of each run, Pallas kernels for 33% -> 34%
where the time goes in v3:
time: 47.3 us; the launch traced here: 46.9 us
  Pallas kernels  19.1 us (40%)
  starting transfers between devices  16.7 us (35%)
  waiting for transfers between devices  5.77 us (12%)
  other arithmetic  2.88 us (6%)
  local copies, waits for them, and re-layouts  1.71 us (4%)
  between operations  0.75 us (2%)
    pallas_call x9, Pallas kernels, call(): pl.pallas_call(kernel, name=name, out_shape=outs, in_specs=[SMEM if x.dty...  19.1 us
    ppermute x8, starting transfers between devices, rotate(): lax.ppermute(value, axis, [(i, (i + by) % size) for i in range(size)])  16.7 us
    ppermute x8, waiting for transfers between devices, rotate(): lax.ppermute(value, axis, [(i, (i + by) % size) for i in range(size)])  5.77 us
    select_n x2, other arithmetic, side_by_side(): jnp.where(left, lax.pad(one, zero, ((0, 0, 0), (0, lanes, 0))), lax.pad(o...  2.74 us
  transfers between devices with their start and end apart: 8, of which 3 were waited for; matrix products, arithmetic and copies ran while one was open for 6% of the time, Pallas kernels for 34%

profile of v3, /device:TPU:123, one launch (start us, length us, event | category | flops | bytes accessed | tf_op | source)
XLA Modules:
  0.0 46.9 jit_solution(18204566143914193138)
XLA Ops:
  0.6 1.0 %pad_select_fusion.1.own_ref.refs_1_.refs_4_ = bf16[384,256]{1,0:T(8,128)(2,1)S(1)} fusion(bf16[384,128]{1,0:T(8,128)(2,1)} %param.7, bf16[384,128]{1,0:T(8,128)(2,1)} %param.6, pred[256]{0:T(512)(128)(4,1)S(1)} %iota_compare_fusion.1), kind=kLoop, calls=%fused_computation.3 | loop fusion | flops 98304 | bytes 393472 | tf_op jit(solution)/shard_map/jit(_where)/select_n | solution.py:368
  1.6 3.6 %collective-permute-start.2 = (bf16[384,256]{1,0:T(8,128)(2,1)S(1)}, bf16[384,256]{1,0:T(8,128)(2,1)S(1)}, u32[]{:S(2)}, u32[]{:S(2)}) collective-permute-start(bf16[384,256]{1,0:T(8,128)(2,1)S(1)} %pad_select_fusion.1.own_ref.refs_1_.refs_4_), channel_id=1, source_target_pairs={{0,1},{1,2},{2,3},{3,4},{4,5},{5,6},{6,7},{7,8},{8,9},{9,10},{10,1... | collective-permute-start | bytes 589832 | tf_op jit(solution)/shard_map/ppermute | solution.py:361
  5.2 0.9 %fusion.1 = (s32[2]{0:T(128)S(1)}, s32[2]{0:T(128)S(1)}, s32[2]{0:T(128)S(1)}, s32[2]{0:T(128)S(1)}, s32[2]{0:T(128)S(1)}) fusion(s32[512]{0:T(512)} %param.9, s32[]{:T(128)S(6)} %select_n.55, s32[]{:T(128)S(6)} %select_n.51, s32[]{:T(128)S(6)} %select_n.49, s32[]{:T(128)S(6)} %select_n.47, s32[]{:T(128)S(6)} %select_n.53), kind=kLoop, calls=%fused_computation.7 | loop fusion | bytes 100 | tf_op jit(solution)/shard_map/dynamic_slice | solution.py:382
  6.2 0.1 concatenate.3.spans_ref
  6.2 0.6 %again.1 = (bf16[384,256]{1,0:T(8,128)(2,1)S(1)}, f32[16,768]{1,0:T(8,128)S(1)}) custom-call(s32[10]{0:T(128)S(1)} %concatenate.3.spans_ref, bf16[384,256]{1,0:T(8,128)(2,1)S(1)} %pad_select_fusion.1.own_ref.refs_1_.refs_4_), custom_call_target="tpu_custom_call" | custom-call | tf_op jit(solution)/shard_map/again/pallas_call | solution.py:264
  6.8 1.4 %collective-permute-start.1 = (bf16[384,256]{1,0:T(8,128)(2,1)S(1)}, bf16[384,256]{1,0:T(8,128)(2,1)S(1)}, u32[]{:S(2)}, u32[]{:S(2)}) collective-permute-start(bf16[384,256]{1,0:T(8,128)(2,1)S(1)} %get-tuple-element.40), channel_id=1, source_target_pairs={{0,16},{16,32},{32,48},{48,64},{64,80},{80,96},{96,112},{112,128},... | collective-permute-start | bytes 589832 | tf_op jit(solution)/shard_map/ppermute | solution.py:361
  8.2 0.7 %collective-permute-start = (bf16[384,256]{1,0:T(8,128)(2,1)S(1)}, bf16[384,256]{1,0:T(8,128)(2,1)S(1)}, u32[]{:S(2)}, u32[]{:S(2)}) collective-permute-start(bf16[384,256]{1,0:T(8,128)(2,1)S(1)} %get-tuple-element.40), channel_id=1, source_target_pairs={{0,2},{1,3},{2,4},{3,5},{4,6},{5,7},{6,8},{7,9},{8,10},{9,11},{10,... | collective-permute-start | bytes 589832 | tf_op jit(solution)/shard_map/ppermute | solution.py:361
  9.0 1.8 %pad_select_fusion.refs_0_ = bf16[384,2048]{1,0:T(8,128)(2,1)S(1)} fusion(bf16[384,1024]{1,0:T(8,128)(2,1)} %param.8, bf16[384,1024]{1,0:T(8,128)(2,1)} %param.5, pred[2048]{0:T(1024)(128)(4,1)S(1)} %iota_compare_fusion), kind=kLoop, calls=%fused_computation | loop fusion | flops 786432 | bytes 3147776 | tf_op jit(solution)/shard_map/jit(_where)/select_n | solution.py:368
  10.7 2.3 %own_scores.1 = (bf16[4,768,128]{2,1,0:T(8,128)(2,1)S(1)}, bf16[4,768,128]{2,1,0:T(8,128)(2,1)S(1)}, bf16[4,128,768]{2,1,0:T(8,128)(2,1)S(1)}, bf16[4,128,768]{2...) custom-call(f32[16,768]{1,0:T(8,128)S(1)} %get-tuple-element.34.bias, ...), custom_call_target="tpu_custom_call" | custom-call | flops 1207959552 | tf_op jit(solution)/shard_map/own_scores/pallas_call | solution.py:264
  13.1 0.0 collective-permute-done.2.refs_3_.refs_5_
  13.1 0.8 %collective-permute-start.3 = (bf16[384,256]{1,0:T(8,128)(2,1)S(1)}, bf16[384,256]{1,0:T(8,128)(2,1)S(1)}, u32[]{:S(2)}, u32[]{:S(2)}) collective-permute-start(bf16[384,256]{1,0:T(8,128)(2,1)S(1)} %collective-permute-done.2.refs_3_.refs_5_), channel_id=1, source_target_pairs={{0,2},{1,3},{2,4},{3,5},{4,6},{5,7},{6,8},{7,9},{8,10},{9,11},{10,... | collective-permute-start | bytes 589832 | tf_op jit(solution)/shard_map/ppermute | solution.py:361
  13.9 1.6 %first_scores.1 = (bf16[4,384,768]{2,1,0:T(8,128)(2,1)S(1)}, bf16[4,384,768]{2,1,0:T(8,128)(2,1)S(1)}, f32[4,8,768]{2,1,0:T(8,128)S(1)}) custom-call(f32[16,768]{1,0:T(8,128)S(1)} %get-tuple-element.34.bias_ref, bf16[4,128,768]{2,1,0:T(8,128)(2,1)S(1)} %get-tuple-element.37.refs_0_.qt_ref, bf16[4,128,768]{2,1,0:T(8,128)(2,1)S(1)} %get-tuple-element.38.refs_1_.gt_ref, ...), custom_call_target="tpu_custom_call" | custom-call | flops 1207959552 | tf_op jit(solution)/shard_map/first_scores/pallas_call | solution.py:264
  15.5 0.0 collective-permute-done.1.refs_4_.refs_6_
  15.5 0.0 collective-permute-done.refs_3_.refs_7_
  15.5 3.0 %two_scores.1 = (bf16[4,768,768]{2,1,0:T(8,128)(2,1)S(1)}, bf16[4,768,768]{2,1,0:T(8,128)(2,1)S(1)}, f32[4,8,768]{2,1,0:T(8,128)S(1)}) custom-call(f32[16,768]{1,0:T(8,128)S(1)} %get-tuple-element.34.bias_ref, bf16[4,128,768]{2,1,0:T(8,128)(2,1)S(1)} %get-tuple-element.37.refs_0_.qt_ref, bf16[4,128,768]{2,1,0:T(8,128)(2,1)S(1)} %get-tuple-element.38.refs_1_.gt_ref, ...), custom_call_target="tpu_custom_call" | custom-call | flops 2415919104 | tf_op jit(solution)/shard_map/two_scores/pallas_call | solution.py:264
  18.5 1.2 %collective-permute-done.3.kv_ref.refs_8_ = bf16[384,256]{1,0:T(8,128)(2,1)S(1)} collective-permute-done((bf16[384,256]{1,0:T(8,128)(2,1)S(1)}, bf16[384,256]{1,0:T(8,128)(2,1)S(1)}, u32[]{:S(2)}, u32[]{:S(2)}) %collective-permute-start.3) | collective-permute-done | bytes 196640 | tf_op jit(solution)/shard_map/ppermute | solution.py:361
  19.7 3.0 %last_block.1 = (f32[4,8,768]{2,1,0:T(8,128)S(1)}, bf16[4,384,768]{2,1,0:T(8,128)(2,1)S(1)}, bf16[384,256]{1,0:T(8,128)(2,1)S(1)}) custom-call(f32[16,768]{1,0:T(8,128)S(1)} %get-tuple-element.34.bias_ref, bf16[4,768,128]{2,1,0:T(8,128)(2,1)S(1)} %get-tuple-element.35.q_ref, bf16[4,768,128]{2,1,0:T(8,128)(2,1)S(1)} %get-tuple-element.36.go_ref, ...), custom_call_target="tpu_custom_call" | custom-call | flops 2415919104 | tf_op jit(solution)/shard_map/last_block/pallas_call | solution.py:264
  22.7 0.8 %collective-permute-start.4 = (bf16[384,256]{1,0:T(8,128)(2,1)S(1)}, bf16[384,256]{1,0:T(8,128)(2,1)S(1)}, u32[]{:S(2)}, u32[]{:S(2)}) collective-permute-start(bf16[384,256]{1,0:T(8,128)(2,1)S(1)} %get-tuple-element.62), channel_id=1, source_target_pairs={{0,14},{1,15},{2,0},{3,1},{4,2},{5,3},{6,4},{7,5},{8,6},{9,7},{10,... | collective-permute-start | bytes 589832 | tf_op jit(solution)/shard_map/ppermute | solution.py:361
  23.5 1.4 %outer_grads.1 = (bf16[4,384,768]{2,1,0:T(8,128)(2,1)S(1)}, bf16[384,256]{1,0:T(8,128)(2,1)S(1)}) custom-call(bf16[4,768,128]{2,1,0:T(8,128)(2,1)S(1)} %get-tuple-element.35.q_ref, bf16[4,768,128]{2,1,0:T(8,128)(2,1)S(1)} %get-tuple-element.36.go_ref, f32[4,8,768]{2,1,0:T(8,128)S(1)} %get-tuple-element.44.rates, ...), custom_call_target="tpu_custom_call" | custom-call | flops 1207959552 | tf_op jit(solution)/shard_map/outer_grads/pallas_call | solution.py:264
  24.9 1.4 %second_grads.1 = (bf16[4,384,768]{2,1,0:T(8,128)(2,1)S(1)}, bf16[384,256]{1,0:T(8,128)(2,1)S(1)}) custom-call(bf16[4,768,128]{2,1,0:T(8,128)(2,1)S(1)} %get-tuple-element.35.q_ref, bf16[4,768,128]{2,1,0:T(8,128)(2,1)S(1)} %get-tuple-element.36.go_ref, f32[4,8,768]{2,1,0:T(8,128)S(1)} %get-tuple-element.44.rates, ...), custom_call_target="tpu_custom_call" | custom-call | flops 1207959552 | tf_op jit(solution)/shard_map/second_grads/pallas_call | solution.py:264
  26.3 0.1 collective-permute-start.6
  26.4 1.1 %collective-permute-start.7 = (bf16[384,256]{1,0:T(8,128)(2,1)S(1)}, bf16[384,256]{1,0:T(8,128)(2,1)S(1)}, u32[]{:S(2)}, u32[]{:S(2)}) collective-permute-start(bf16[384,256]{1,0:T(8,128)(2,1)S(1)} %get-tuple-element.64), channel_id=1, source_target_pairs={{0,240},{16,0},{32,16},{48,32},{64,48},{80,64},{96,80},{112,96},{1... | collective-permute-start | bytes 589832 | tf_op jit(solution)/shard_map/ppermute | solution.py:361
  27.5 1.4 %first_grads.1 = (bf16[4,384,768]{2,1,0:T(8,128)(2,1)S(1)}, bf16[384,256]{1,0:T(8,128)(2,1)S(1)}) custom-call(bf16[4,768,128]{2,1,0:T(8,128)(2,1)S(1)} %get-tuple-element.35.q_ref, bf16[4,768,128]{2,1,0:T(8,128)(2,1)S(1)} %get-tuple-element.36.go_ref, f32[4,8,768]{2,1,0:T(8,128)S(1)} %get-tuple-element.44.rates, ...), custom_call_target="tpu_custom_call" | custom-call | flops 1207959552 | tf_op jit(solution)/shard_map/first_grads/pallas_call | solution.py:264
  29.0 0.7 %collective-permute-done.4 = bf16[384,256]{1,0:T(8,128)(2,1)S(1)} collective-permute-done((bf16[384,256]{1,0:T(8,128)(2,1)S(1)}, bf16[384,256]{1,0:T(8,128)(2,1)S(1)}, u32[]{:S(2)}, u32[]{:S(2)}) %collective-permute-start.4) | collective-permute-done | bytes 196640 | tf_op jit(solution)/shard_map/ppermute | solution.py:361
  29.7 8.1 %collective-permute-start.5 = (bf16[384,256]{1,0:T(8,128)(2,1)S(1)}, bf16[384,256]{1,0:T(8,128)(2,1)S(1)}, u32[]{:S(2)}, u32[]{:S(2)}) collective-permute-start(bf16[384,256]{1,0:T(8,128)(2,1)S(1)} %add_convert_fusion.1), channel_id=1, source_target_pairs={{0,15},{1,0},{2,1},{3,2},{4,3},{5,4},{6,5},{7,6},{8,7},{9,8},{10,9... | collective-permute-start | bytes 589832 | tf_op jit(solution)/shard_map/ppermute | solution.py:361
  37.8 4.4 %own_grads.1 = (bf16[384,1024]{1,0:T(8,128)(2,1)}, f32[384,256]{1,0:T(8,128)S(1)}) custom-call(bf16[4,768,128]{2,1,0:T(8,128)(2,1)S(1)} %get-tuple-element.35.q_ref, bf16[4,768,128]{2,1,0:T(8,128)(2,1)S(1)} %get-tuple-element.36.go_ref, f32[4,8,768]{2,1,0:T(8,128)S(1)} %get-tuple-element.44.rates, f32[4,8,768]{2,1,0:T(8,128)S(1)} %get-tuple-element.42.refs_5_.refs_0_.near, ...), custom_call_target="tpu_custom_call" | custom-call | flops 6039797760 | tf_op jit(solution)/shard_map/own_grads/pallas_call | solution.py:264
  42.3 0.0 collective-permute-done.6
  42.3 0.0 collective-permute-done.7
  42.3 3.8 %collective-permute-done.5 = bf16[384,256]{1,0:T(8,128)(2,1)S(1)} collective-permute-done((bf16[384,256]{1,0:T(8,128)(2,1)S(1)}, bf16[384,256]{1,0:T(8,128)(2,1)S(1)}, u32[]{:S(2)}, u32[]{:S(2)}) %collective-permute-start.5) | collective-permute-done | bytes 196640 | tf_op jit(solution)/shard_map/ppermute | solution.py:361
  46.1 0.1 add_convert_fusion
  46.2 0.7 %fusion = (bf16[384,128]{1,0:T(8,128)(2,1)}, bf16[384,128]{1,0:T(8,128)(2,1)}) fusion(bf16[384,256]{1,0:T(8,128)(2,1)S(1)} %add_convert_fusion), kind=kLoop, calls=%fused_computation.6 | loop fusion | bytes 393216 | tf_op jit(solution)/shard_map/slice | solution.py:406
  (3 shorter events, 0.1 us)
Async XLA Ops:
  1.6 11.5 %collective-permute-start.2 = (bf16[384,256]{1,0:T(8,128)(2,1)S(1)}, bf16[384,256]{1,0:T(8,128)(2,1)S(1)}, u32[]{:S(2)}, u32[]{:S(2)}) collective-permute-start(bf16[384,256]{1,0:T(8,128)(2,1)S(1)} %pad_select_fusion.1.own_ref.refs_1_.refs_4_), channel_id=1, source_target_pairs={{0,1},{1,2},{2,3},{3,4},{4,5},{5,6},{6,7},{7,8},{8,9},{9,10},{10,1... | collective-permute-start | bytes 589832 | tf_op jit(solution)/shard_map/ppermute | solution.py:361
  6.8 8.6 %collective-permute-start.1 = (bf16[384,256]{1,0:T(8,128)(2,1)S(1)}, bf16[384,256]{1,0:T(8,128)(2,1)S(1)}, u32[]{:S(2)}, u32[]{:S(2)}) collective-permute-start(bf16[384,256]{1,0:T(8,128)(2,1)S(1)} %get-tuple-element.40), channel_id=1, source_target_pairs={{0,16},{16,32},{32,48},{48,64},{64,80},{80,96},{96,112},{112,128},... | collective-permute-start | bytes 589832 | tf_op jit(solution)/shard_map/ppermute | solution.py:361
  8.2 7.2 %collective-permute-start = (bf16[384,256]{1,0:T(8,128)(2,1)S(1)}, bf16[384,256]{1,0:T(8,128)(2,1)S(1)}, u32[]{:S(2)}, u32[]{:S(2)}) collective-permute-start(bf16[384,256]{1,0:T(8,128)(2,1)S(1)} %get-tuple-element.40), channel_id=1, source_target_pairs={{0,2},{1,3},{2,4},{3,5},{4,6},{5,7},{6,8},{7,9},{8,10},{9,11},{10,... | collective-permute-start | bytes 589832 | tf_op jit(solution)/shard_map/ppermute | solution.py:361
  13.1 6.6 %collective-permute-start.3 = (bf16[384,256]{1,0:T(8,128)(2,1)S(1)}, bf16[384,256]{1,0:T(8,128)(2,1)S(1)}, u32[]{:S(2)}, u32[]{:S(2)}) collective-permute-start(bf16[384,256]{1,0:T(8,128)(2,1)S(1)} %collective-permute-done.2.refs_3_.refs_5_), channel_id=1, source_target_pairs={{0,2},{1,3},{2,4},{3,5},{4,6},{5,7},{6,8},{7,9},{8,10},{9,11},{10,... | collective-permute-start | bytes 589832 | tf_op jit(solution)/shard_map/ppermute | solution.py:361
  22.7 6.9 %collective-permute-start.4 = (bf16[384,256]{1,0:T(8,128)(2,1)S(1)}, bf16[384,256]{1,0:T(8,128)(2,1)S(1)}, u32[]{:S(2)}, u32[]{:S(2)}) collective-permute-start(bf16[384,256]{1,0:T(8,128)(2,1)S(1)} %get-tuple-element.62), channel_id=1, source_target_pairs={{0,14},{1,15},{2,0},{3,1},{4,2},{5,3},{6,4},{7,5},{8,6},{9,7},{10,... | collective-permute-start | bytes 589832 | tf_op jit(solution)/shard_map/ppermute | solution.py:361
  26.3 16.0 %collective-permute-start.6 = (bf16[384,256]{1,0:T(8,128)(2,1)S(1)}, bf16[384,256]{1,0:T(8,128)(2,1)S(1)}, u32[]{:S(2)}, u32[]{:S(2)}) collective-permute-start(bf16[384,256]{1,0:T(8,128)(2,1)S(1)} %get-tuple-element.63), channel_id=1, source_target_pairs={{0,14},{1,15},{2,0},{3,1},{4,2},{5,3},{6,4},{7,5},{8,6},{9,7},{10,... | collective-permute-start | bytes 589832 | tf_op jit(solution)/shard_map/ppermute | solution.py:361
  26.4 15.9 %collective-permute-start.7 = (bf16[384,256]{1,0:T(8,128)(2,1)S(1)}, bf16[384,256]{1,0:T(8,128)(2,1)S(1)}, u32[]{:S(2)}, u32[]{:S(2)}) collective-permute-start(bf16[384,256]{1,0:T(8,128)(2,1)S(1)} %get-tuple-element.64), channel_id=1, source_target_pairs={{0,240},{16,0},{32,16},{48,32},{64,48},{80,64},{96,80},{112,96},{1... | collective-permute-start | bytes 589832 | tf_op jit(solution)/shard_map/ppermute | solution.py:361
  29.7 16.4 %collective-permute-start.5 = (bf16[384,256]{1,0:T(8,128)(2,1)S(1)}, bf16[384,256]{1,0:T(8,128)(2,1)S(1)}, u32[]{:S(2)}, u32[]{:S(2)}) collective-permute-start(bf16[384,256]{1,0:T(8,128)(2,1)S(1)} %add_convert_fusion.1), channel_id=1, source_target_pairs={{0,15},{1,0},{2,1},{3,2},{4,3},{5,4},{6,5},{7,6},{8,7},{9,8},{10,9... | collective-permute-start | bytes 589832 | tf_op jit(solution)/shard_map/ppermute | solution.py:361
